TPU v7x, 32 devices: a whole 2x2x4 slice. The times are simulated.
32 devices in a mesh: grp: 2 (over y), tm: 16 (over z, x, core).
Axes of the slice: x: 2, y: 2, z: 4, core: 2. Of those that a mesh axis runs over, the one named last changes fastest.
Arguments:
- residual: bfloat16 [4, 2, 4096, 2048], P('grp', None, 'tm'), parts along dimension 0, may hold values from -6 to 6
- eigenbasis: bfloat16 [2048, 2048], P('tm'), may hold values from -0.125 to 0.125
- eigenvalues: float32 [2048], replicated, may hold values from 0.05 to 5
- node_order: int32 [2048], replicated, may hold values from 0 to 2047, each once
Outputs:
- correction: float32 [4, 2, 4096, 2048], P('grp', None, 'tm'), parts along dimension 0
There are 2 independent parts, one for each index of `grp`. A program takes and returns all parts, laid end to end along the dimension named above; an argument that names none is the same for every part. Nothing has to cross between parts.
Inputs may be any that keep to these rules, and one draw needn't show every extreme that they name: node_order names every number of 0 to 2047 exactly once.
All inputs are finite; a program needn't handle non-finite values.
Results may differ from a plain program's by a relative error of at most 0.0055.
Values may be sent and summed in bfloat16 or wider, within the bound.
A program may use at most 64 MiB of HBM per device.

v0:
```python
import jax
import jax.numpy as jnp
from jax import lax
from jax.sharding import PartitionSpec as P


def sine_block(length, first_col, block_width):
    row_index = jnp.arange(length, dtype=jnp.int32)[:, None] + 1
    col_index = first_col + jnp.arange(block_width, dtype=jnp.int32)[None, :] + 1
    phase_mod = row_index * col_index % (2 * (length + 1))
    angle_rad = phase_mod.astype(jnp.float32) * (jnp.pi / (length + 1))
    return (jnp.sqrt(2.0 / (length + 1)) * jnp.sin(angle_rad)).astype(jnp.bfloat16)


def on_device(residual, eigenbasis, eigenvalues, node_order):
    num_vectors, fields, time_local, states = residual.shape
    length = time_local * lax.axis_size("tm")
    inverse = jnp.zeros_like(node_order).at[node_order].set(jnp.arange(states, dtype=jnp.int32))
    ordered = jnp.take(residual, node_order, axis=3)
    modal_data = jnp.einsum(
        "sj,rfts->rftj",
        lax.all_gather(eigenbasis, "tm", axis=0, tiled=True),
        ordered,
        preferred_element_type=jnp.float32,
    ).astype(jnp.bfloat16)
    spread = lax.all_to_all(modal_data, "tm", split_axis=3, concat_axis=2, tiled=True)
    mode_count = spread.shape[3]
    offset = lax.axis_index("tm") * mode_count
    local_mu = lax.dynamic_slice_in_dim(eigenvalues, offset, mode_count, 0)
    block_width = min(256, length)

    def one_block(block_index, accumulated):
        first_col = block_index * block_width
        sine_table = sine_block(length, first_col, block_width)
        spectral = jnp.einsum(
            "rftj,tk->rfjk", spread, sine_table, preferred_element_type=jnp.float32
        )
        freq_index = (first_col + jnp.arange(block_width, dtype=jnp.int32) + 1).astype(jnp.float32)
        time_eigen = 4.0 * jnp.sin(freq_index * (jnp.pi / (2 * (length + 1)))) ** 2
        shift_sum = local_mu[:, None] + time_eigen[None, :]
        determinant = shift_sum * shift_sum + 1.0
        state_part = (shift_sum * spectral[:, 0] - spectral[:, 1]) / determinant
        adjoint = (spectral[:, 0] + shift_sum * spectral[:, 1]) / determinant
        scaled = jnp.stack((state_part, adjoint), axis=1).astype(jnp.bfloat16)
        return accumulated + jnp.einsum(
            "rfjk,tk->rfjt", scaled, sine_table, preferred_element_type=jnp.float32
        )

    zero_modes = jnp.zeros((num_vectors, fields, mode_count, length), jnp.float32)
    accumulated = lax.fori_loop(0, length // block_width, one_block, zero_modes)
    back_modes = accumulated.astype(jnp.bfloat16)
    returned = lax.all_to_all(back_modes, "tm", split_axis=3, concat_axis=2, tiled=True)
    shaped = jnp.einsum(
        "sj,rfjt->rfts",
        lax.all_gather(eigenbasis, "tm", axis=0, tiled=True),
        returned,
        preferred_element_type=jnp.float32,
    )
    return jnp.take(shaped, inverse, axis=3)


def solution(mesh):
    placed = (P("grp", None, "tm", None), P("tm", None), P(), P())
    return jax.shard_map(
        on_device, mesh=mesh, in_specs=placed, out_specs=P("grp", None, "tm", None), check_vma=False
    )
```

profile of v0, /device:TPU:0, one launch (start us, length us, event | category | flops | bytes accessed | tf_op | source)
XLA Modules:
  0.0 1123.7 jit_solution(11743297354848499549)
XLA Ops:
  18.4 24.6 %gather_fusion = bf16[2048,2,2,256]{3,2,1,0:T(2,128)(2,1)} fusion(bf16[2,2,256,2048]{2,1,3,0:T(2,128)(2,1)} %copy.19, s32[2048]{0:T(1024)S(1)} %get-tuple-element.145), kind=kCustom, calls=%fused_computation | custom fusion | bytes 8396800 | tf_op jit(solution)/shard_map/jit(_take)/gather | solution.py:19
  52.3 34.9 %all-gather.2.cloned.1.call-done = bf16[2048,2048]{1,0:T(8,128)(2,1)} async-done(((bf16[128,2048]{1,0:T(8,128)(2,1)}), bf16[2048,2048]{1,0:T(8,128)(2,1)}) %all-gather.2.cloned.1.call-update) | async-done | bytes 8388624 | tf_op jit(solution)/shard_map/all_gather | solution.py:22
  117.7 76.8 %all-to-all-done = bf16[2,2,256,2048]{2,1,0,3:T(2,128)(2,1)} async-done(((bf16[2,2,256,2048]{2,1,0,3:T(2,128)(2,1)}), bf16[2,2,256,2048]{2,1,0,3:T(2,128)(2,1)}, u32[]{:S(2)}, u32[]{:S(2)}) %all-to-all-start) | async-done | bytes 4194336 | tf_op jit(solution)/shard_map/all_to_all | solution.py:26
  205.7 709.7 %while.16 = (s32[]{:T(128)}, f32[2,2,128,4096]{3,2,1,0:T(8,128)}, f32[128]{0:T(128)S(1)}, bf16[2,2,4096,128]{3,2,1,0:T(8,128)(2,1)}, s32[]{:T(128)}, /*index=5*/s32[]{:T(128)}, s32[]{:T(128)}) while((s32[]{:T(128)}, f32[2,2,128,4096]{3,2,1,0:T(8,128)}, f32[128]{0:T(128)S(1)}, bf16[2,2,4096,128]{3,2,1,0:T(8,128)(2,1)}, s32[]{:T(128)}, ...), condition=%wide.region_2.3_spmd.clone, body=%wide.region_1.2_spmd.clone.sunk | while | flops 2175506432 | bytes 23123560 | solution.py:50
  205.7 22.2 %fusion.58 = f32[2,2,128,256]{2,3,1,0:T(8,128)S(1)} fusion(bf16[2,2,4096,128]{3,2,1,0:T(8,128)(2,1)} %get-tuple-element.196, s32[256]{0:T(256)S(1)} %add_add_fusion.2, s32[4096]{0:T(1024)S(1)} %iota_add_fusion.2), kind=kOutput, calls=%fused_computation.22.clone.1 | convolution fusion | flops 1085276160 | bytes 4736000 | tf_op jit(solution)/shard_map/while/body/eval_jaxpr/rftj,tk->rfjk/dot_general | solution.py:35
  248.9 22.2 %fusion.58 = f32[2,2,128,256]{2,3,1,0:T(8,128)S(1)} fusion(bf16[2,2,4096,128]{3,2,1,0:T(8,128)(2,1)} %get-tuple-element.196, s32[256]{0:T(256)S(1)} %add_add_fusion.2, s32[4096]{0:T(1024)S(1)} %iota_add_fusion.2), kind=kOutput, calls=%fused_computation.22.clone.1 | convolution fusion | flops 1085276160 | bytes 4736000 | tf_op jit(solution)/shard_map/while/body/eval_jaxpr/rftj,tk->rfjk/dot_general | solution.py:35
  271.4 22.0 %select_add_fusion.2 = f32[2,2,128,4096]{3,2,1,0:T(8,128)} fusion(f32[2,2,128,4096]{3,2,1,0:T(8,128)} %get-tuple-element.187, pred[]{:T(512)S(6)} %compare.3, s32[256]{0:T(256)S(1)} %add_add_fusion.2, s32[4096]{0:T(1024)S(1)} %iota_add_fusion.2, bf16[2,1,128,256]{2,3,1,0:T(8,128)(2,1)S(1)} %get-tuple-element.177, ...), kind=kOutput, calls=%fused_computation.3.clone.1 | convolution fusion | flops 1089601536 | bytes 17056768 | tf_op jit(solution)/shard_map/while/body/eval_jaxpr/rfjk,tk->rfjt/dot_general | solution.py:45
  293.4 22.2 %fusion.58 = f32[2,2,128,256]{2,3,1,0:T(8,128)S(1)} fusion(bf16[2,2,4096,128]{3,2,1,0:T(8,128)(2,1)} %get-tuple-element.196, s32[256]{0:T(256)S(1)} %add_add_fusion.2, s32[4096]{0:T(1024)S(1)} %iota_add_fusion.2), kind=kOutput, calls=%fused_computation.22.clone.1 | convolution fusion | flops 1085276160 | bytes 4736000 | tf_op jit(solution)/shard_map/while/body/eval_jaxpr/rftj,tk->rfjk/dot_general | solution.py:35
  315.8 22.0 %select_add_fusion.2 = f32[2,2,128,4096]{3,2,1,0:T(8,128)} fusion(f32[2,2,128,4096]{3,2,1,0:T(8,128)} %get-tuple-element.187, pred[]{:T(512)S(6)} %compare.3, s32[256]{0:T(256)S(1)} %add_add_fusion.2, s32[4096]{0:T(1024)S(1)} %iota_add_fusion.2, bf16[2,1,128,256]{2,3,1,0:T(8,128)(2,1)S(1)} %get-tuple-element.177, ...), kind=kOutput, calls=%fused_computation.3.clone.1 | convolution fusion | flops 1089601536 | bytes 17056768 | tf_op jit(solution)/shard_map/while/body/eval_jaxpr/rfjk,tk->rfjt/dot_general | solution.py:45
  337.8 22.2 %fusion.58 = f32[2,2,128,256]{2,3,1,0:T(8,128)S(1)} fusion(bf16[2,2,4096,128]{3,2,1,0:T(8,128)(2,1)} %get-tuple-element.196, s32[256]{0:T(256)S(1)} %add_add_fusion.2, s32[4096]{0:T(1024)S(1)} %iota_add_fusion.2), kind=kOutput, calls=%fused_computation.22.clone.1 | convolution fusion | flops 1085276160 | bytes 4736000 | tf_op jit(solution)/shard_map/while/body/eval_jaxpr/rftj,tk->rfjk/dot_general | solution.py:35
  360.3 22.0 %select_add_fusion.2 = f32[2,2,128,4096]{3,2,1,0:T(8,128)} fusion(f32[2,2,128,4096]{3,2,1,0:T(8,128)} %get-tuple-element.187, pred[]{:T(512)S(6)} %compare.3, s32[256]{0:T(256)S(1)} %add_add_fusion.2, s32[4096]{0:T(1024)S(1)} %iota_add_fusion.2, bf16[2,1,128,256]{2,3,1,0:T(8,128)(2,1)S(1)} %get-tuple-element.177, ...), kind=kOutput, calls=%fused_computation.3.clone.1 | convolution fusion | flops 1089601536 | bytes 17056768 | tf_op jit(solution)/shard_map/while/body/eval_jaxpr/rfjk,tk->rfjt/dot_general | solution.py:45
  382.2 22.2 %fusion.58 = f32[2,2,128,256]{2,3,1,0:T(8,128)S(1)} fusion(bf16[2,2,4096,128]{3,2,1,0:T(8,128)(2,1)} %get-tuple-element.196, s32[256]{0:T(256)S(1)} %add_add_fusion.2, s32[4096]{0:T(1024)S(1)} %iota_add_fusion.2), kind=kOutput, calls=%fused_computation.22.clone.1 | convolution fusion | flops 1085276160 | bytes 4736000 | tf_op jit(solution)/shard_map/while/body/eval_jaxpr/rftj,tk->rfjk/dot_general | solution.py:35
  404.7 22.0 %select_add_fusion.2 = f32[2,2,128,4096]{3,2,1,0:T(8,128)} fusion(f32[2,2,128,4096]{3,2,1,0:T(8,128)} %get-tuple-element.187, pred[]{:T(512)S(6)} %compare.3, s32[256]{0:T(256)S(1)} %add_add_fusion.2, s32[4096]{0:T(1024)S(1)} %iota_add_fusion.2, bf16[2,1,128,256]{2,3,1,0:T(8,128)(2,1)S(1)} %get-tuple-element.177, ...), kind=kOutput, calls=%fused_computation.3.clone.1 | convolution fusion | flops 1089601536 | bytes 17056768 | tf_op jit(solution)/shard_map/while/body/eval_jaxpr/rfjk,tk->rfjt/dot_general | solution.py:45
  426.6 22.2 %fusion.58 = f32[2,2,128,256]{2,3,1,0:T(8,128)S(1)} fusion(bf16[2,2,4096,128]{3,2,1,0:T(8,128)(2,1)} %get-tuple-element.196, s32[256]{0:T(256)S(1)} %add_add_fusion.2, s32[4096]{0:T(1024)S(1)} %iota_add_fusion.2), kind=kOutput, calls=%fused_computation.22.clone.1 | convolution fusion | flops 1085276160 | bytes 4736000 | tf_op jit(solution)/shard_map/while/body/eval_jaxpr/rftj,tk->rfjk/dot_general | solution.py:35
  471.1 22.2 %fusion.58 = f32[2,2,128,256]{2,3,1,0:T(8,128)S(1)} fusion(bf16[2,2,4096,128]{3,2,1,0:T(8,128)(2,1)} %get-tuple-element.196, s32[256]{0:T(256)S(1)} %add_add_fusion.2, s32[4096]{0:T(1024)S(1)} %iota_add_fusion.2), kind=kOutput, calls=%fused_computation.22.clone.1 | convolution fusion | flops 1085276160 | bytes 4736000 | tf_op jit(solution)/shard_map/while/body/eval_jaxpr/rftj,tk->rfjk/dot_general | solution.py:35
  493.5 22.0 %select_add_fusion.2 = f32[2,2,128,4096]{3,2,1,0:T(8,128)} fusion(f32[2,2,128,4096]{3,2,1,0:T(8,128)} %get-tuple-element.187, pred[]{:T(512)S(6)} %compare.3, s32[256]{0:T(256)S(1)} %add_add_fusion.2, s32[4096]{0:T(1024)S(1)} %iota_add_fusion.2, bf16[2,1,128,256]{2,3,1,0:T(8,128)(2,1)S(1)} %get-tuple-element.177, ...), kind=kOutput, calls=%fused_computation.3.clone.1 | convolution fusion | flops 1089601536 | bytes 17056768 | tf_op jit(solution)/shard_map/while/body/eval_jaxpr/rfjk,tk->rfjt/dot_general | solution.py:45
  515.5 22.2 %fusion.58 = f32[2,2,128,256]{2,3,1,0:T(8,128)S(1)} fusion(bf16[2,2,4096,128]{3,2,1,0:T(8,128)(2,1)} %get-tuple-element.196, s32[256]{0:T(256)S(1)} %add_add_fusion.2, s32[4096]{0:T(1024)S(1)} %iota_add_fusion.2), kind=kOutput, calls=%fused_computation.22.clone.1 | convolution fusion | flops 1085276160 | bytes 4736000 | tf_op jit(solution)/shard_map/while/body/eval_jaxpr/rftj,tk->rfjk/dot_general | solution.py:35
  538.0 22.0 %select_add_fusion.2 = f32[2,2,128,4096]{3,2,1,0:T(8,128)} fusion(f32[2,2,128,4096]{3,2,1,0:T(8,128)} %get-tuple-element.187, pred[]{:T(512)S(6)} %compare.3, s32[256]{0:T(256)S(1)} %add_add_fusion.2, s32[4096]{0:T(1024)S(1)} %iota_add_fusion.2, bf16[2,1,128,256]{2,3,1,0:T(8,128)(2,1)S(1)} %get-tuple-element.177, ...), kind=kOutput, calls=%fused_computation.3.clone.1 | convolution fusion | flops 1089601536 | bytes 17056768 | tf_op jit(solution)/shard_map/while/body/eval_jaxpr/rfjk,tk->rfjt/dot_general | solution.py:45
  559.9 22.2 %fusion.58 = f32[2,2,128,256]{2,3,1,0:T(8,128)S(1)} fusion(bf16[2,2,4096,128]{3,2,1,0:T(8,128)(2,1)} %get-tuple-element.196, s32[256]{0:T(256)S(1)} %add_add_fusion.2, s32[4096]{0:T(1024)S(1)} %iota_add_fusion.2), kind=kOutput, calls=%fused_computation.22.clone.1 | convolution fusion | flops 1085276160 | bytes 4736000 | tf_op jit(solution)/shard_map/while/body/eval_jaxpr/rftj,tk->rfjk/dot_general | solution.py:35
  604.4 22.2 %fusion.58 = f32[2,2,128,256]{2,3,1,0:T(8,128)S(1)} fusion(bf16[2,2,4096,128]{3,2,1,0:T(8,128)(2,1)} %get-tuple-element.196, s32[256]{0:T(256)S(1)} %add_add_fusion.2, s32[4096]{0:T(1024)S(1)} %iota_add_fusion.2), kind=kOutput, calls=%fused_computation.22.clone.1 | convolution fusion | flops 1085276160 | bytes 4736000 | tf_op jit(solution)/shard_map/while/body/eval_jaxpr/rftj,tk->rfjk/dot_general | solution.py:35
  648.8 22.2 %fusion.58 = f32[2,2,128,256]{2,3,1,0:T(8,128)S(1)} fusion(bf16[2,2,4096,128]{3,2,1,0:T(8,128)(2,1)} %get-tuple-element.196, s32[256]{0:T(256)S(1)} %add_add_fusion.2, s32[4096]{0:T(1024)S(1)} %iota_add_fusion.2), kind=kOutput, calls=%fused_computation.22.clone.1 | convolution fusion | flops 1085276160 | bytes 4736000 | tf_op jit(solution)/shard_map/while/body/eval_jaxpr/rftj,tk->rfjk/dot_general | solution.py:35
  671.3 22.0 %select_add_fusion.2 = f32[2,2,128,4096]{3,2,1,0:T(8,128)} fusion(f32[2,2,128,4096]{3,2,1,0:T(8,128)} %get-tuple-element.187, pred[]{:T(512)S(6)} %compare.3, s32[256]{0:T(256)S(1)} %add_add_fusion.2, s32[4096]{0:T(1024)S(1)} %iota_add_fusion.2, bf16[2,1,128,256]{2,3,1,0:T(8,128)(2,1)S(1)} %get-tuple-element.177, ...), kind=kOutput, calls=%fused_computation.3.clone.1 | convolution fusion | flops 1089601536 | bytes 17056768 | tf_op jit(solution)/shard_map/while/body/eval_jaxpr/rfjk,tk->rfjt/dot_general | solution.py:45
  693.2 22.2 %fusion.58 = f32[2,2,128,256]{2,3,1,0:T(8,128)S(1)} fusion(bf16[2,2,4096,128]{3,2,1,0:T(8,128)(2,1)} %get-tuple-element.196, s32[256]{0:T(256)S(1)} %add_add_fusion.2, s32[4096]{0:T(1024)S(1)} %iota_add_fusion.2), kind=kOutput, calls=%fused_computation.22.clone.1 | convolution fusion | flops 1085276160 | bytes 4736000 | tf_op jit(solution)/shard_map/while/body/eval_jaxpr/rftj,tk->rfjk/dot_general | solution.py:35
  715.7 22.0 %select_add_fusion.2 = f32[2,2,128,4096]{3,2,1,0:T(8,128)} fusion(f32[2,2,128,4096]{3,2,1,0:T(8,128)} %get-tuple-element.187, pred[]{:T(512)S(6)} %compare.3, s32[256]{0:T(256)S(1)} %add_add_fusion.2, s32[4096]{0:T(1024)S(1)} %iota_add_fusion.2, bf16[2,1,128,256]{2,3,1,0:T(8,128)(2,1)S(1)} %get-tuple-element.177, ...), kind=kOutput, calls=%fused_computation.3.clone.1 | convolution fusion | flops 1089601536 | bytes 17056768 | tf_op jit(solution)/shard_map/while/body/eval_jaxpr/rfjk,tk->rfjt/dot_general | solution.py:45
  737.7 22.2 %fusion.58 = f32[2,2,128,256]{2,3,1,0:T(8,128)S(1)} fusion(bf16[2,2,4096,128]{3,2,1,0:T(8,128)(2,1)} %get-tuple-element.196, s32[256]{0:T(256)S(1)} %add_add_fusion.2, s32[4096]{0:T(1024)S(1)} %iota_add_fusion.2), kind=kOutput, calls=%fused_computation.22.clone.1 | convolution fusion | flops 1085276160 | bytes 4736000 | tf_op jit(solution)/shard_map/while/body/eval_jaxpr/rftj,tk->rfjk/dot_general | solution.py:35
  782.1 22.2 %fusion.58 = f32[2,2,128,256]{2,3,1,0:T(8,128)S(1)} fusion(bf16[2,2,4096,128]{3,2,1,0:T(8,128)(2,1)} %get-tuple-element.196, s32[256]{0:T(256)S(1)} %add_add_fusion.2, s32[4096]{0:T(1024)S(1)} %iota_add_fusion.2), kind=kOutput, calls=%fused_computation.22.clone.1 | convolution fusion | flops 1085276160 | bytes 4736000 | tf_op jit(solution)/shard_map/while/body/eval_jaxpr/rftj,tk->rfjk/dot_general | solution.py:35
  804.5 22.0 %select_add_fusion.2 = f32[2,2,128,4096]{3,2,1,0:T(8,128)} fusion(f32[2,2,128,4096]{3,2,1,0:T(8,128)} %get-tuple-element.187, pred[]{:T(512)S(6)} %compare.3, s32[256]{0:T(256)S(1)} %add_add_fusion.2, s32[4096]{0:T(1024)S(1)} %iota_add_fusion.2, bf16[2,1,128,256]{2,3,1,0:T(8,128)(2,1)S(1)} %get-tuple-element.177, ...), kind=kOutput, calls=%fused_computation.3.clone.1 | convolution fusion | flops 1089601536 | bytes 17056768 | tf_op jit(solution)/shard_map/while/body/eval_jaxpr/rfjk,tk->rfjt/dot_general | solution.py:45
  826.5 22.2 %fusion.58 = f32[2,2,128,256]{2,3,1,0:T(8,128)S(1)} fusion(bf16[2,2,4096,128]{3,2,1,0:T(8,128)(2,1)} %get-tuple-element.196, s32[256]{0:T(256)S(1)} %add_add_fusion.2, s32[4096]{0:T(1024)S(1)} %iota_add_fusion.2), kind=kOutput, calls=%fused_computation.22.clone.1 | convolution fusion | flops 1085276160 | bytes 4736000 | tf_op jit(solution)/shard_map/while/body/eval_jaxpr/rftj,tk->rfjk/dot_general | solution.py:35
  849.0 22.0 %select_add_fusion.2 = f32[2,2,128,4096]{3,2,1,0:T(8,128)} fusion(f32[2,2,128,4096]{3,2,1,0:T(8,128)} %get-tuple-element.187, pred[]{:T(512)S(6)} %compare.3, s32[256]{0:T(256)S(1)} %add_add_fusion.2, s32[4096]{0:T(1024)S(1)} %iota_add_fusion.2, bf16[2,1,128,256]{2,3,1,0:T(8,128)(2,1)S(1)} %get-tuple-element.177, ...), kind=kOutput, calls=%fused_computation.3.clone.1 | convolution fusion | flops 1089601536 | bytes 17056768 | tf_op jit(solution)/shard_map/while/body/eval_jaxpr/rfjk,tk->rfjt/dot_general | solution.py:45
  870.9 22.2 %fusion.58 = f32[2,2,128,256]{2,3,1,0:T(8,128)S(1)} fusion(bf16[2,2,4096,128]{3,2,1,0:T(8,128)(2,1)} %get-tuple-element.196, s32[256]{0:T(256)S(1)} %add_add_fusion.2, s32[4096]{0:T(1024)S(1)} %iota_add_fusion.2), kind=kOutput, calls=%fused_computation.22.clone.1 | convolution fusion | flops 1085276160 | bytes 4736000 | tf_op jit(solution)/shard_map/while/body/eval_jaxpr/rftj,tk->rfjk/dot_general | solution.py:35
  955.6 69.6 %all-to-all-done.1 = bf16[2,2,128,4096]{2,1,0,3:T(2,128)(2,1)} async-done(((bf16[2,2,128,4096]{2,1,0,3:T(2,128)(2,1)}), bf16[2,2,128,4096]{2,1,0,3:T(2,128)(2,1)}, u32[]{:S(2)}, u32[]{:S(2)}) %all-to-all-start.1) | async-done | bytes 4194336 | tf_op jit(solution)/shard_map/all_to_all | solution.py:52
  1067.1 26.8 %gather_fusion.1 = f32[2048,2,2,256]{3,2,1,0:T(2,128)} fusion(f32[2,2,256,2048]{2,1,3,0:T(2,128)} %copy.25, s32[2048]{0:T(1024)S(1)} %fusion.44), kind=kCustom, calls=%fused_computation.1 | custom fusion | bytes 16785408 | tf_op jit(solution)/shard_map/jit(_take)/gather | solution.py:59
  (112 shorter events, 302.3 us)
Async XLA Ops:
  6.5 80.6 %all-gather.2.cloned.1.call-start = ((), (), s32[]{:S(2)}) async-start(), calls=%async_computation.2 | async-start | bytes 8912896 | tf_op jit(solution)/shard_map/all_gather | solution.py:22
  7.3 11.1 copy-start
  112.4 82.1 %all-to-all-start = ((bf16[2,2,256,2048]{2,1,0,3:T(2,128)(2,1)}), bf16[2,2,256,2048]{2,1,0,3:T(2,128)(2,1)}, u32[]{:S(2)}, u32[]{:S(2)}) async-start(bf16[2,2,256,2048]{2,1,0,3:T(2,128)(2,1)} %copy.21), calls=%async_computation | async-start | bytes 8388608 | tf_op jit(solution)/shard_map/all_to_all | solution.py:26
  927.8 97.3 %all-to-all-start.1 = ((bf16[2,2,128,4096]{2,1,0,3:T(2,128)(2,1)}), bf16[2,2,128,4096]{2,1,0,3:T(2,128)(2,1)}, u32[]{:S(2)}, u32[]{:S(2)}) async-start(bf16[2,2,128,4096]{2,1,0,3:T(2,128)(2,1)} %copy.23), calls=%async_computation.1 | async-start | bytes 8388608 | tf_op jit(solution)/shard_map/all_to_all | solution.py:52
Sparse Core Ops, SparseCore 0:
  9.5 77.5 all-gather.1
where the time goes:
time: 1140 us; the launch traced here: 1120 us
  matrix products  734 us (64%)
  waiting for transfers between devices  182 us (16%)
  local copies, waits for them, and re-layouts  147 us (13%)
  starting transfers between devices  24.2 us (2%)
  other arithmetic  23 us (2%)
  between operations  13.5 us (1%)
    dot_general x16, matrix products, one_block(): jnp.einsum('rftj,tk->rfjk', spread, sine_table, preferred_element_type=jn...  355 us
    dot_general x16, matrix products, one_block(): jnp.einsum('rfjk,tk->rfjt', scaled, sine_table, preferred_element_type=jn...  350 us
    all_to_all x1, waiting for transfers between devices, on_device(): lax.all_to_all(modal_data, 'tm', split_axis=3, concat_axis=2, tiled=True)  76.8 us
    all_to_all x1, waiting for transfers between devices, on_device(): lax.all_to_all(back_modes, 'tm', split_axis=3, concat_axis=2, tiled=True)  69.6 us
    all_gather x1, waiting for transfers between devices, on_device(): lax.all_gather(eigenbasis, 'tm', axis=0, tiled=True)  34.9 us
    gather x1, local copies, waits for them, and re-layouts, on_device(): return jnp.take(shaped, inverse, axis=3)  26.8 us
    gather x1, local copies, waits for them, and re-layouts, on_device(): ordered = jnp.take(residual, node_order, axis=3)  24.6 us
  transfers between devices with their start and end apart: 3, of which 3 were waited for; matrix products, arithmetic and copies ran while one was open for 5% of the time, Pallas kernels for 0%

commit v1 on v0

v1 whole, which is shorter than its diff:
```python
import functools

import jax
import jax.numpy as jnp
from jax import lax
from jax.experimental import pallas as pl
from jax.experimental.pallas import tpu as pltpu
from jax.sharding import PartitionSpec as P

SEGMENTS = 8


def mul(a, b):
    return a[0] * b[0] - a[1] * b[1], a[0] * b[1] + a[1] * b[0]


def add(a, b):
    return a[0] + b[0], a[1] + b[1]


def sub(a, b):
    return a[0] - b[0], a[1] - b[1]


def inverse_of(a):
    size = a[0] * a[0] + a[1] * a[1]
    return a[0] / size, -a[1] / size


def power(a, exponent):
    result, square = None, a
    while exponent:
        if exponent & 1:
            result = square if result is None else mul(result, square)
        exponent >>= 1
        if exponent:
            square = mul(square, square)
    return result


def decay_root(mu):
    wide = 2.0 + mu
    disc_re, disc_im = wide * wide - 5.0, -2.0 * wide
    size = jnp.sqrt(disc_re * disc_re + disc_im * disc_im)
    sqrt_re = jnp.sqrt(0.5 * (size + disc_re))
    sqrt_im = 0.5 * disc_im / sqrt_re
    half = inverse_of((wide + sqrt_re, sqrt_im - 1.0))
    return 2.0 * half[0], 2.0 * half[1]


def carries_kernel(modal_ref, mu_ref, perm_ref, zp_ref, seg_ref, dev_ref, z_ref):
    vectors, _, steps, width = modal_ref.shape
    per_seg = steps // SEGMENTS
    root = decay_root(mu_ref[...])
    root8 = tuple(jnp.broadcast_to(x, (SEGMENTS, width)) for x in root)
    jump = power(root, per_seg)
    for r in range(vectors):
        for f in range(2):
            rows = jnp.dot(perm_ref[...], modal_ref[r, f], preferred_element_type=jnp.float32)
            z_ref[r, f] = rows
            zp_ref[r, f] = rows.astype(jnp.bfloat16)
    for r in range(vectors):
        def at(k):
            here = pl.ds(k * SEGMENTS, SEGMENTS)
            return z_ref[r, 0, here, :], z_ref[r, 1, here, :]

        ahead, behind = at(0), at(per_seg - 1)
        for k in range(1, per_seg):
            ahead = add(at(k), mul(root8, ahead))
            behind = add(at(per_seg - 1 - k), mul(root8, behind))
        for c in range(2):
            seg_ref[r, 0, c] = ahead[c]
            seg_ref[r, 1, c] = behind[c]
        row = lambda a, s: (a[0][s:s + 1], a[1][s:s + 1])
        front, back = row(ahead, 0), row(behind, SEGMENTS - 1)
        for s in range(1, SEGMENTS):
            front = add(row(ahead, s), mul(jump, front))
            back = add(row(behind, SEGMENTS - 1 - s), mul(jump, back))
        for c in range(2):
            dev_ref[r, 0, c] = front[c]
            dev_ref[r, 1, c] = back[c]


def solve_kernel(zp_ref, seg_ref, edge_ref, mu_ref, perm_ref, out_ref, p_ref, u_ref):
    vectors, _, steps, width = zp_ref.shape
    per_seg = steps // SEGMENTS
    root = decay_root(mu_ref[...])
    root8 = tuple(jnp.broadcast_to(x, (SEGMENTS, width)) for x in root)
    jump = power(root, per_seg)
    square = mul(root, root)
    gain = mul(root, inverse_of((1.0 - square[0], -square[1])))
    for r in range(vectors):
        row = lambda a, s: (seg_ref[r, a, 0, s:s + 1, :], seg_ref[r, a, 1, s:s + 1, :])
        lefts = [(edge_ref[r, 0, 0], edge_ref[r, 0, 1])]
        rights = [(edge_ref[r, 1, 0], edge_ref[r, 1, 1])]
        for s in range(SEGMENTS):
            lefts.append(add(row(0, s), mul(jump, lefts[-1])))
        for s in range(SEGMENTS - 1, 0, -1):
            rights.append(add(row(1, s), mul(jump, rights[-1])))
        rights = rights[::-1]
        ends = [mul(gain, add(rights[s], mul(root, lefts[s + 1]))) for s in range(SEGMENTS)]
        stack = lambda rows: tuple(jnp.concatenate([x[c] for x in rows], axis=0) for c in range(2))
        p = stack(lefts[:SEGMENTS])
        for k in range(0, per_seg, 2):
            both = pl.ds(k * SEGMENTS, 2 * SEGMENTS)
            pair = [zp_ref[r, f, both, :].astype(jnp.float32) for f in range(2)]
            for h in range(2):
                z = tuple(x[h * SEGMENTS:(h + 1) * SEGMENTS] for x in pair)
                p = add(z, mul(root8, p))
                for c in range(2):
                    p_ref[c, pl.ds((k + h) * SEGMENTS, SEGMENTS), :] = p[c]
        u = stack(ends)
        for k in range(per_seg - 2, -1, -2):
            later = []
            for h in (1, 0):
                here = pl.ds((k + h) * SEGMENTS, SEGMENTS)
                u = mul(root8, add((p_ref[0, here, :], p_ref[1, here, :]), u))
                later.append(u)
            both = pl.ds(k * SEGMENTS, 2 * SEGMENTS)
            for c in range(2):
                u_ref[c, both, :] = jnp.concatenate([later[1][c], later[0][c]], axis=0).astype(jnp.bfloat16)
        for c in range(2):
            out_ref[r, c] = jnp.dot(perm_ref[...], u_ref[c], preferred_element_type=jnp.float32).astype(jnp.bfloat16)


def on_device(residual, eigenbasis, eigenvalues, node_order):
    vectors, fields, steps, states = residual.shape
    modes = eigenbasis.shape[1]
    parts = lax.axis_size("tm")
    me = lax.axis_index("tm")
    per_seg = steps // SEGMENTS
    width = min(256, modes)
    blocks = modes // width

    inverse = jnp.zeros_like(node_order).at[node_order].set(jnp.arange(states, dtype=jnp.int32), unique_indices=True)
    basis = lax.all_gather(eigenbasis, "tm", axis=0, tiled=True)
    basis = jnp.take(basis, inverse, axis=0, mode="clip", unique_indices=True)

    modal = jnp.einsum("rfts,sj->rftj", residual, basis, preferred_element_type=jnp.float32).astype(jnp.bfloat16)

    row = jnp.arange(steps, dtype=jnp.int32)
    time_of_row = (row % SEGMENTS) * per_seg + row // SEGMENTS
    perm = (time_of_row[:, None] == row[None, :]).astype(jnp.bfloat16)
    mu = eigenvalues[None, :]

    f32 = jnp.float32
    wide_block = pl.BlockSpec((vectors, fields, steps, width), lambda j: (0, 0, 0, j))
    seg_block = pl.BlockSpec((vectors, 2, 2, SEGMENTS, width), lambda j: (0, 0, 0, 0, j))
    dev_block = pl.BlockSpec((vectors, 2, 2, 1, width), lambda j: (0, 0, 0, 0, j))
    mu_block = pl.BlockSpec((1, width), lambda j: (0, j))
    perm_block = pl.BlockSpec((steps, steps), lambda j: (0, 0))
    params = pltpu.CompilerParams(vmem_limit_bytes=40 * 1024 * 1024)
    zp, seg, dev = pl.pallas_call(
        carries_kernel,
        grid=(blocks,),
        in_specs=[wide_block, mu_block, perm_block],
        out_specs=[wide_block, seg_block, dev_block],
        out_shape=[
            jax.ShapeDtypeStruct((vectors, fields, steps, modes), jnp.bfloat16),
            jax.ShapeDtypeStruct((vectors, 2, 2, SEGMENTS, modes), f32),
            jax.ShapeDtypeStruct((vectors, 2, 2, 1, modes), f32),
        ],
        scratch_shapes=[pltpu.VMEM((vectors, fields, steps, width), f32)],
        compiler_params=params,
        name="carries",
    )(modal, mu, perm)

    every = lax.all_gather(dev[:, :, :, 0, :], "tm", axis=0, tiled=False)
    root = decay_root(mu)
    hop = power(root, steps)
    zero = (jnp.zeros((vectors, modes), f32),) * 2
    pick = lambda keep, new, old: tuple(jnp.where(keep, a, b) for a, b in zip(new, old))
    left, right, all_left, all_right = zero, zero, zero, zero
    from_start = from_end = (jnp.ones_like(mu), jnp.zeros_like(mu))
    for d in range(parts):
        e = parts - 1 - d
        all_left = add((every[d, :, 0, 0], every[d, :, 0, 1]), mul(hop, all_left))
        all_right = add((every[e, :, 1, 0], every[e, :, 1, 1]), mul(hop, all_right))
        left = pick(d < me, all_left, left)
        right = pick(e > me, all_right, right)
        from_start = pick(d < me, mul(hop, from_start), from_start)
        from_end = pick(e > me, mul(hop, from_end), from_end)
    whole = mul(power(hop, parts), root)
    whole_sq = mul(whole, whole)
    scale = mul(root, inverse_of((1.0 - whole_sq[0], -whole_sq[1])))
    start_term = mul(scale, sub(all_right, mul(whole, all_left)))
    end_term = mul(scale, sub(all_left, mul(whole, all_right)))
    left = sub(left, mul(start_term, from_start))
    right = sub(right, mul(end_term, from_end))
    edge = jnp.stack((jnp.stack(left, 1), jnp.stack(right, 1)), 1)[:, :, :, None, :]

    back = pl.pallas_call(
        solve_kernel,
        grid=(blocks,),
        in_specs=[wide_block, seg_block, dev_block, mu_block, perm_block],
        out_specs=wide_block,
        out_shape=jax.ShapeDtypeStruct((vectors, fields, steps, modes), jnp.bfloat16),
        scratch_shapes=[
            pltpu.VMEM((2, steps, width), f32),
            pltpu.VMEM((2, steps, width), jnp.bfloat16),
        ],
        compiler_params=params,
        name="solve",
    )(zp, seg, edge, mu, perm.T)

    return jnp.einsum("rftj,sj->rfts", back, basis, preferred_element_type=jnp.float32)


def solution(mesh):
    placed = (P("grp", None, "tm", None), P("tm", None), P(), P())
    return jax.shard_map(
        on_device, mesh=mesh, in_specs=placed, out_specs=P("grp", None, "tm", None), check_vma=False
    )
```

time: 1140 us -> 197 us (0.17); the launches traced: 1120 us -> 197 us
  matrix products: 734 us -> 23.9 us
  local copies, waits for them, and re-layouts: 147 us -> 33.9 us
  waiting for transfers between devices: 182 us -> 108 us
  starting transfers between devices: 24.2 us -> 0.04 us
  other arithmetic: 23 us -> 3.6 us
  Pallas kernels: 0 us -> 13.9 us
    dot_general x34 -> x2, matrix products: 734 us -> 23.9 us  [the longest x1 12.5 us: on_device(): jnp.einsum('rfts,sj->rftj', residual, basis, preferred_element_type=jnp.f...]
    all_to_all x2 -> x0, waiting for transfers between devices: 146 us -> none  [the longest x1 76.8 us: on_device(): lax.all_to_all(modal_data, 'tm', split_axis=3, concat_axis=2, tiled=True)]
    all_gather x1 -> x2, waiting for transfers between devices: 34.9 us -> 107 us  [the longest x1 71 us: on_device(): basis = lax.all_gather(eigenbasis, 'tm', axis=0, tiled=True)]
    gather x2 -> x1, local copies, waits for them, and re-layouts: 51.4 us -> 21 us  [on_device(): basis = jnp.take(basis, inverse, axis=0, mode='clip', unique_indices=True)]
    all_to_all x3 -> x0, local copies, waits for them, and re-layouts: 25.3 us -> none  [the longest x2 14.2 us: on_device(): lax.all_to_all(back_modes, 'tm', split_axis=3, concat_axis=2, tiled=True)]
    all_to_all x2 -> x0, starting transfers between devices: 24.2 us -> none  [the longest x1 19.7 us: on_device(): lax.all_to_all(back_modes, 'tm', split_axis=3, concat_axis=2, tiled=True)]
    select_n x2 -> x3, other arithmetic: 19.1 us -> 0.23 us  [on_device(): jnp.where(keep, a, b)]
    pallas_call x0 -> x2, Pallas kernels: none -> 13.9 us  [the longest x1 7.78 us: on_device(): pl.pallas_call(solve_kernel, grid=(blocks,), in_specs=[wide_block, seg_bl...]
  transfers between devices with their start and end apart: 3 -> 2, of which waited for: 3 -> 2; matrix products, arithmetic and copies ran while one was open for 5% -> 5% of each run, Pallas kernels for 0% -> 0%
where the time goes in v1:
time: 197 us
  waiting for transfers between devices  108 us (55%)
  local copies, waits for them, and re-layouts  33.9 us (17%)
  matrix products  23.9 us (12%)
  Pallas kernels  13.9 us (7%)
  between operations  13.6 us (7%)
  other arithmetic  3.6 us (2%)
    all_gather x1, waiting for transfers between devices, on_device(): basis = lax.all_gather(eigenbasis, 'tm', axis=0, tiled=True)  71 us
    all_gather x1, waiting for transfers between devices, on_device(): every = lax.all_gather(dev[:, :, :, 0, :], 'tm', axis=0, tiled=False)  36 us
    gather x1, local copies, waits for them, and re-layouts, on_device(): basis = jnp.take(basis, inverse, axis=0, mode='clip', unique_indices=True)  21 us
    dot_general x1, matrix products, on_device(): jnp.einsum('rfts,sj->rftj', residual, basis, preferred_element_type=jnp.f...  12.5 us
    dot_general x1, matrix products, on_device(): jnp.einsum('rftj,sj->rfts', back, basis, preferred_element_type=jnp.float32)  11.3 us
    scatter x1, local copies, waits for them, and re-layouts, on_device(): jnp.zeros_like(node_order).at[node_order]  8.04 us
    pallas_call x1, Pallas kernels, on_device(): pl.pallas_call(solve_kernel, grid=(blocks,), in_specs=[wide_block, seg_bl...  7.78 us
    pallas_call x1, Pallas kernels, on_device(): pl.pallas_call(carries_kernel, grid=(blocks,), in_specs=[wide_block, mu_b...  6.09 us
  transfers between devices with their start and end apart: 2, of which 2 were waited for; matrix products, arithmetic and copies ran while one was open for 5% of the time, Pallas kernels for 0%

profile of v1, /device:TPU:0, one launch (start us, length us, event | category | flops | bytes accessed | tf_op | source)
XLA Modules:
  0.0 196.6 jit_solution(12486282617306115427)
XLA Ops:
  6.5 0.0 all-gather.4.cloned.1.call-start
  6.5 0.7 all-gather.4.cloned.1.call-update
  7.3 0.0 all-gather.6.cloned.1.call-start
  7.3 0.7 compare_select_fusion
  8.0 8.0 %scatter_custom_fusion = s32[2048]{0:T(1024)S(1)} fusion(s32[2048]{0:T(1024)S(1)} %compare_select_fusion, s32[2048]{0:T(1024)S(1)} %iota.14, s32[]{:T(128)} %constant.27.clone.1), kind=kCustom, calls=%fused_computation.322 | custom fusion | bytes 8196 | tf_op jit(solution)/shard_map/scatter | solution.py:135
  16.1 0.1 fusion.7
  16.2 71.0 %all-gather.4.cloned.1.call-done = bf16[2048,2048]{1,0:T(8,128)(2,1)} async-done(((bf16[128,2048]{1,0:T(8,128)(2,1)}), bf16[2048,2048]{1,0:T(8,128)(2,1)}) %all-gather.4.cloned.1.call-update) | async-done | bytes 8388624 | tf_op jit(solution)/shard_map/all_gather | solution.py:136
  87.1 21.0 %gather_fusion = bf16[2048,2048]{1,0:T(8,128)(2,1)} fusion(bf16[2048,2048]{1,0:T(8,128)(2,1)} %all-gather.4.cloned.1.call-done, s32[2048]{0:T(1024)S(1)} %broadcast_clamp_fusion), kind=kCustom, calls=%fused_computation | custom fusion | bytes 16785408 | tf_op jit(solution)/shard_map/jit(_take)/gather | solution.py:137
  108.1 0.0 copy-start.2
  108.1 12.5 %convert_bitcast_fusion.modal_ref = bf16[2,2,256,2048]{3,2,1,0:T(8,128)(2,1)S(1)} fusion(bf16[2,2,256,2048]{3,2,1,0:T(8,128)(2,1)} %param.4, bf16[2048,2048]{1,0:T(8,128)(2,1)} %gather_fusion), kind=kOutput, calls=%fused_computation.6 | convolution fusion | flops 8592031744 | bytes 16777216 | tf_op jit(solution)/shard_map/rfts,sj->rftj/dot_general | solution.py:139
  120.6 0.0 copy-done.2
  120.7 6.1 %carries.1 = (bf16[2,2,256,2048]{3,2,1,0:T(8,128)(2,1)S(1)}, f32[2,2,2,8,2048]{4,3,2,1,0:T(8,128)S(1)}, f32[2,2,2,1,2048]{4,3,2,1,0:T(1,128)S(1)}) custom-call(bf16[2,2,256,2048]{3,2,1,0:T(8,128)(2,1)S(1)} %convert_bitcast_fusion.modal_ref, f32[1,2048]{1,0:T(1,128)S(1)} %bitcast.370, bf16[256,256]{1,0:T(8,128)(2,1)S(1)} %get-tuple-element.85.perm_ref), custom_call_target="tpu_custom_call" | custom-call | tf_op jit(solution)/shard_map/carries/pallas_call | solution.py:153
  126.8 0.0 copy-start
  126.8 2.0 copy-done
  128.7 0.7 copy.11
  129.4 0.0 all-gather.6.cloned.1.call-update
  129.5 0.1 subtract_select_fusion.14
  129.6 0.1 add_select_fusion.15
  129.7 0.1 subtract_select_fusion
  129.8 36.0 %all-gather.6.cloned.1.call-done = f32[32,2,2,1,2048]{4,2,3,1,0:T(2,128)} async-done(((f32[2,2,2,1,2048]{4,2,3,1,0:T(2,128)}), f32[32,2,2,1,2048]{4,2,3,1,0:T(2,128)}) %all-gather.6.cloned.1.call-update) | async-done | bytes 1048592 | tf_op jit(solution)/shard_map/all_gather | solution.py:168
  165.8 0.0 copy-start.1
  165.8 2.2 %copy.12 = f32[32,2,2,1,2048]{4,1,2,0,3:T(2,128)S(1)} copy(f32[32,2,2,1,2048]{4,2,3,1,0:T(2,128)} %all-gather.6.cloned.1.call-done) | data formatting | bytes 2097152 | tf_op jit(solution)/shard_map/all_gather | solution.py:168
  168.0 0.5 fusion.74
  168.5 1.2 fusion.8
  169.7 0.2 fusion.9
  169.9 0.2 fusion.11
  170.2 0.2 fusion.10
  170.4 0.1 maximum_bitcast_fusion
  170.6 0.0 copy-done.1
  170.6 7.8 %solve.1 = bf16[2,2,256,2048]{3,2,1,0:T(8,128)(2,1)S(1)} custom-call(bf16[2,2,256,2048]{3,2,1,0:T(8,128)(2,1)S(1)} %copy-done.1, f32[2,2,2,8,2048]{4,3,2,1,0:T(8,128)S(1)} %get-tuple-element.9.seg_ref, f32[2,2,2,1,2048]{4,3,2,1,0:T(1,128)S(1)} %broadcast_in_dim.26.edge_ref, f32[1,2048]{1,0:T(1,128)S(1)} %bitcast.371, ...), custom_call_target="tpu_custom_call" | custom-call | tf_op jit(solution)/shard_map/solve/pallas_call | solution.py:192
  178.4 0.0 copy-done.3
  178.4 11.3 %fusion = f32[2,2,256,2048]{3,2,1,0:T(8,128)} fusion(bf16[2,2,256,2048]{3,2,1,0:T(8,128)(2,1)S(1)} %solve.1, bf16[2048,2048]{1,0:T(8,128)(2,1)S(1)} %copy-done.3), kind=kOutput, calls=%fused_computation.2 | convolution fusion | flops 8589934592 | bytes 20971520 | tf_op jit(solution)/shard_map/rftj,sj->rfts/dot_general | solution.py:206
  (8 shorter events, 0.1 us)
Async XLA Ops:
  6.5 80.6 %all-gather.4.cloned.1.call-start = ((), (), s32[]{:S(2)}) async-start(), calls=%async_computation | async-start | bytes 8912896 | tf_op jit(solution)/shard_map/all_gather | solution.py:136
  7.3 158.5 %all-gather.6.cloned.1.call-start = ((), (), s32[]{:S(2)}) async-start(), calls=%async_computation.1 | async-start | bytes 1114112 | tf_op jit(solution)/shard_map/all_gather | solution.py:168
  108.1 12.5 %copy-start.2 = (f32[2048]{0:T(1024)S(1)}, f32[2048]{0:T(1024)}, u32[]{:S(2)}) copy-start(f32[2048]{0:T(1024)} %param.6) | copy-start | bytes 24580
  126.8 2.0 %copy-start = (bf16[2,2,256,2048]{3,2,1,0:T(8,128)(2,1)}, bf16[2,2,256,2048]{3,2,1,0:T(8,128)(2,1)S(1)}, u32[]{:S(2)}) copy-start(bf16[2,2,256,2048]{3,2,1,0:T(8,128)(2,1)S(1)} %get-tuple-element.8.zp_ref) | copy-start | bytes 12582916
  165.8 4.8 %copy-start.1 = (bf16[2,2,256,2048]{3,2,1,0:T(8,128)(2,1)S(1)}, bf16[2,2,256,2048]{3,2,1,0:T(8,128)(2,1)}, u32[]{:S(2)}) copy-start(bf16[2,2,256,2048]{3,2,1,0:T(8,128)(2,1)} %copy-done) | copy-start | bytes 12582916
  165.8 12.6 %copy-start.3 = (bf16[2048,2048]{1,0:T(8,128)(2,1)S(1)}, bf16[2048,2048]{1,0:T(8,128)(2,1)}, u32[]{:S(2)}) copy-start(bf16[2048,2048]{1,0:T(8,128)(2,1)} %gather_fusion) | copy-start | bytes 25165828
Sparse Core Ops, SparseCore 0:
  9.5 77.5 all-gather.3
  129.5 36.1 all-gather.5

commit v2 on v1

--- a/solution.py
+++ b/solution.py
@@ -123,6 +123,92 @@
             out_ref[r, c] = jnp.dot(perm_ref[...], u_ref[c], preferred_element_type=jnp.float32).astype(jnp.bfloat16)
 
 
+def gather_kernel(chips, mine_ref, node_ref, out_ref, held, send_sem, recv_sem, pair_send, pair_recv):
+    _, _, rows, modes = held.shape
+    states = out_ref.shape[0]
+    half = modes // 2
+    tile = min(256, states)
+    me = lax.axis_index("tm")
+    core, chip = me % 2, me // 2
+    odd = chip % 2
+    place = (1 - odd) * (chip // 2) + odd * (chips - 1 - chip // 2)
+
+    def chip_at(position):
+        position = (position + chips) % chips
+        second = position // (chips // 2)
+        return (1 - second) * 2 * position + second * (2 * (chips - 1 - position) + 1)
+
+    targets = (chip_at(place + 1) * 2 + core, chip_at(place - 1) * 2 + core)
+    pair = chip * 2 + 1 - core
+
+    def piece(step, h):
+        source = chip_at(place - step if h == 0 else place + step)
+        return source, held.at[source, core, :, pl.ds(h * half, half)]
+
+    def ring(step, h):
+        _, ref = piece(step, h)
+        return pltpu.make_async_remote_copy(
+            src_ref=ref, dst_ref=ref, send_sem=send_sem.at[step, h], recv_sem=recv_sem.at[step, h],
+            device_id={"tm": targets[h]}, device_id_type=pl.DeviceIdType.MESH,
+        )
+
+    def share(step, h):
+        _, ref = piece(step, h)
+        return pltpu.make_async_remote_copy(
+            src_ref=ref, dst_ref=ref, send_sem=pair_send.at[step, h], recv_sem=pair_recv.at[step, h],
+            device_id={"tm": pair}, device_id_type=pl.DeviceIdType.MESH,
+        )
+
+    def place_rows(step, h, first):
+        source, _ = piece(step, h)
+        nodes = node_ref[source]
+        columns = pl.ds(h * half, half)
+
+        def one_tile(t, carry):
+            start = pl.multiple_of(t * tile, tile)
+            index = lax.broadcasted_iota(jnp.int32, (tile, 2 * rows), 0) + start
+            choose = jnp.where(index == nodes, 1.0, 0.0).astype(jnp.bfloat16)
+            block = held[source, :, :, columns].reshape(2 * rows, half)
+            moved = jnp.dot(choose, block, preferred_element_type=jnp.float32)
+            here = pl.ds(start, tile)
+            if not first:
+                moved = moved + out_ref[here, columns].astype(jnp.float32)
+            out_ref[here, columns] = moved.astype(jnp.bfloat16)
+            return carry
+
+        lax.fori_loop(0, states // tile, one_tile, 0)
+
+    held[chip, core] = mine_ref[...]
+    barrier = pltpu.get_barrier_semaphore()
+    for target in (*targets, pair):
+        pl.semaphore_signal(barrier, inc=1, device_id={"tm": target}, device_id_type=pl.DeviceIdType.MESH)
+    pl.semaphore_wait(barrier, 3)
+
+    def one_step(step, first):
+        for h in range(2):
+            ring(step, h).start()
+        for h in range(2):
+            share(step, h).start()
+        for h in range(2):
+            share(step, h).wait()
+            place_rows(step, h, first)
+        for h in range(2):
+            ring(step, h).wait()
+
+    one_step(0, True)
+
+    def body(step, carry):
+        one_step(step, False)
+        return carry
+
+    lax.fori_loop(1, chips - 1, body, 0)
+    for h in range(2):
+        share(chips - 1, h).start()
+    for h in range(2):
+        share(chips - 1, h).wait()
+        place_rows(chips - 1, h, False)
+
+
 def on_device(residual, eigenbasis, eigenvalues, node_order):
     vectors, fields, steps, states = residual.shape
     modes = eigenbasis.shape[1]
@@ -132,9 +218,20 @@
     width = min(256, modes)
     blocks = modes // width
 
-    inverse = jnp.zeros_like(node_order).at[node_order].set(jnp.arange(states, dtype=jnp.int32), unique_indices=True)
-    basis = lax.all_gather(eigenbasis, "tm", axis=0, tiled=True)
-    basis = jnp.take(basis, inverse, axis=0, mode="clip", unique_indices=True)
+    chips = parts // 2
+    rows = eigenbasis.shape[0]
+    basis = pl.pallas_call(
+        functools.partial(gather_kernel, chips),
+        out_shape=jax.ShapeDtypeStruct((states, modes), jnp.bfloat16),
+        in_specs=[pl.BlockSpec(memory_space=pltpu.VMEM)] * 2,
+        out_specs=pl.BlockSpec(memory_space=pltpu.VMEM),
+        scratch_shapes=[pltpu.VMEM((chips, 2, rows, modes), jnp.bfloat16)]
+        + [pltpu.SemaphoreType.DMA((chips, 2))] * 4,
+        compiler_params=pltpu.CompilerParams(
+            collective_id=0, has_side_effects=True, vmem_limit_bytes=44 * 1024 * 1024
+        ),
+        name="gather_rows",
+    )(eigenbasis, node_order.reshape(chips, 1, 2 * rows))
 
     modal = jnp.einsum("rfts,sj->rftj", residual, basis, preferred_element_type=jnp.float32).astype(jnp.bfloat16)
 
@@ -165,22 +262,29 @@
         name="carries",
     )(modal, mu, perm)
 
-    every = lax.all_gather(dev[:, :, :, 0, :], "tm", axis=0, tiled=False)
     root = decay_root(mu)
     hop = power(root, steps)
+    one = (jnp.ones_like(mu), jnp.zeros_like(mu))
     zero = (jnp.zeros((vectors, modes), f32),) * 2
     pick = lambda keep, new, old: tuple(jnp.where(keep, a, b) for a, b in zip(new, old))
-    left, right, all_left, all_right = zero, zero, zero, zero
-    from_start = from_end = (jnp.ones_like(mu), jnp.zeros_like(mu))
-    for d in range(parts):
-        e = parts - 1 - d
-        all_left = add((every[d, :, 0, 0], every[d, :, 0, 1]), mul(hop, all_left))
-        all_right = add((every[e, :, 1, 0], every[e, :, 1, 1]), mul(hop, all_right))
-        left = pick(d < me, all_left, left)
-        right = pick(e > me, all_right, right)
-        from_start = pick(d < me, mul(hop, from_start), from_start)
-        from_end = pick(e > me, mul(hop, from_end), from_end)
-    whole = mul(power(hop, parts), root)
+    group = dev[:, :, :, 0, :]
+    left, right = zero, zero
+    from_start, from_end, span, reach = one, one, hop, 1
+    while reach < parts:
+        other = lax.ppermute(group, "tm", [(d, d ^ reach) for d in range(parts)])
+        upper = (me // reach) % 2 == 1
+        low, high = jnp.where(upper, other, group), jnp.where(upper, group, other)
+        low_front, high_front = (low[:, 0, 0], low[:, 0, 1]), (high[:, 0, 0], high[:, 0, 1])
+        low_back, high_back = (low[:, 1, 0], low[:, 1, 1]), (high[:, 1, 0], high[:, 1, 1])
+        left = pick(upper, add(left, mul(from_start, low_front)), left)
+        right = pick(upper, right, add(right, mul(from_end, high_back)))
+        from_start = pick(upper, mul(from_start, span), from_start)
+        from_end = pick(upper, from_end, mul(from_end, span))
+        front, back = add(high_front, mul(span, low_front)), add(low_back, mul(span, high_back))
+        group = jnp.stack((jnp.stack(front, 1), jnp.stack(back, 1)), 1)
+        span, reach = mul(span, span), 2 * reach
+    all_left, all_right = (group[:, 0, 0], group[:, 0, 1]), (group[:, 1, 0], group[:, 1, 1])
+    whole = mul(span, root)
     whole_sq = mul(whole, whole)
     scale = mul(root, inverse_of((1.0 - whole_sq[0], -whole_sq[1])))
     start_term = mul(scale, sub(all_right, mul(whole, all_left)))

time: 197 us -> 120 us (0.61)
  waiting for transfers between devices: 108 us -> 11.7 us
  Pallas kernels: 13.9 us -> 74 us
  local copies, waits for them, and re-layouts: 33.9 us -> 4.04 us
  between operations: 13.6 us -> 0.33 us
  starting transfers between devices: 0.04 us -> 4.23 us
    all_gather x2 -> x0, waiting for transfers between devices: 107 us -> none  [the longest x1 71 us: on_device(): basis = lax.all_gather(eigenbasis, 'tm', axis=0, tiled=True)]
    pallas_call x0 -> x1, Pallas kernels: none -> 60.2 us  [on_device(): pl.pallas_call(functools.partial(gather_kernel, chips), out_shape=jax.Sha...]
    gather x1 -> x0, local copies, waits for them, and re-layouts: 21 us -> none  [on_device(): basis = jnp.take(basis, inverse, axis=0, mode='clip', unique_indices=True)]
    ppermute x0 -> x4, waiting for transfers between devices: none -> 11.7 us  [on_device(): other = lax.ppermute(group, 'tm', [(d, d ^ reach) for d in range(parts)])]
    scatter x1 -> x0, local copies, waits for them, and re-layouts: 8.04 us -> none  [on_device(): jnp.zeros_like(node_order).at[node_order]]
    ppermute x0 -> x4, starting transfers between devices: none -> 4.23 us  [on_device(): other = lax.ppermute(group, 'tm', [(d, d ^ reach) for d in range(parts)])]
    dot_general x1, matrix products: 12.5 us -> 9.21 us  [on_device(): jnp.einsum('rfts,sj->rftj', residual, basis, preferred_element_type=jnp.f...]
    all_gather x1 -> x0, local copies, waits for them, and re-layouts: 2.21 us -> none  [on_device(): every = lax.all_gather(dev[:, :, :, 0, :], 'tm', axis=0, tiled=False)]
  transfers between devices with their start and end apart: 2 -> 4, of which waited for: 2 -> 4; matrix products, arithmetic and copies ran while one was open for 5% -> 0% of each run, Pallas kernels for 0% -> 0%
where the time goes in v2:
time: 120 us; the launch traced here: 119 us
  Pallas kernels  74 us (62%)
  matrix products  22.7 us (19%)
  waiting for transfers between devices  11.7 us (10%)
  starting transfers between devices  4.23 us (4%)
  local copies, waits for them, and re-layouts  4.04 us (3%)
  other arithmetic  2.42 us (2%)
    pallas_call x1, Pallas kernels, on_device(): pl.pallas_call(functools.partial(gather_kernel, chips), out_shape=jax.Sha...  60.2 us
    dot_general x1, matrix products, on_device(): jnp.einsum('rftj,sj->rfts', back, basis, preferred_element_type=jnp.float32)  13.5 us
    ppermute x4, waiting for transfers between devices, on_device(): other = lax.ppermute(group, 'tm', [(d, d ^ reach) for d in range(parts)])  11.7 us
    dot_general x1, matrix products, on_device(): jnp.einsum('rfts,sj->rftj', residual, basis, preferred_element_type=jnp.f...  9.21 us
    pallas_call x1, Pallas kernels, on_device(): pl.pallas_call(solve_kernel, grid=(blocks,), in_specs=[wide_block, seg_bl...  7.78 us
    pallas_call x1, Pallas kernels, on_device(): pl.pallas_call(carries_kernel, grid=(blocks,), in_specs=[wide_block, mu_b...  6.09 us
    ppermute x4, starting transfers between devices, on_device(): other = lax.ppermute(group, 'tm', [(d, d ^ reach) for d in range(parts)])  4.23 us
    unnamed x14, local copies, waits for them, and re-layouts  3.76 us
  transfers between devices with their start and end apart: 4, of which 4 were waited for; matrix products, arithmetic and copies ran while one was open for 0% of the time, Pallas kernels for 0%

profile of v2, /device:TPU:0, one launch (start us, length us, event | category | flops | bytes accessed | tf_op | source)
XLA Modules:
  0.0 119.4 jit_solution(4335660422778703958)
XLA Ops:
  0.0 0.1 fusion.7
  0.1 1.0 copy-done.3
  1.2 0.7 copy-done.5
  1.9 60.2 %gather_rows.1 = bf16[2048,2048]{1,0:T(8,128)(2,1)S(1)} custom-call(bf16[128,2048]{1,0:T(8,128)(2,1)S(1)} %copy-done.3, s32[8,1,256]{2,1,0:T(1,128)S(1)} %bitcast.363), custom_call_target="tpu_custom_call" | custom-call | tf_op jit(solution)/shard_map/gather_rows/pallas_call | solution.py:223
  62.1 9.2 %convert_bitcast_fusion.modal_ref = bf16[2,2,256,2048]{3,2,1,0:T(8,128)(2,1)S(1)} fusion(bf16[2,2,256,2048]{3,2,1,0:T(8,128)(2,1)S(1)} %copy-done.6, bf16[2048,2048]{1,0:T(8,128)(2,1)S(1)} %gather_rows.1), kind=kOutput, calls=%fused_computation.4 | convolution fusion | flops 8592031744 | bytes 16777216 | tf_op jit(solution)/shard_map/rfts,sj->rftj/dot_general | solution.py:236
  71.3 6.1 %carries.1 = (bf16[2,2,256,2048]{3,2,1,0:T(8,128)(2,1)S(1)}, f32[2,2,2,8,2048]{4,3,2,1,0:T(8,128)S(1)}, f32[2,2,2,1,2048]{4,3,2,1,0:T(1,128)S(1)}) custom-call(bf16[2,2,256,2048]{3,2,1,0:T(8,128)(2,1)S(1)} %convert_bitcast_fusion.modal_ref, f32[1,2048]{1,0:T(1,128)S(1)} %bitcast.361, bf16[256,256]{1,0:T(8,128)(2,1)S(1)} %get-tuple-element.62.perm_ref), custom_call_target="tpu_custom_call" | custom-call | tf_op jit(solution)/shard_map/carries/pallas_call | solution.py:250
  77.4 2.0 %copy-done.1 = bf16[2,2,256,2048]{3,2,1,0:T(8,128)(2,1)} copy-done((bf16[2,2,256,2048]{3,2,1,0:T(8,128)(2,1)}, bf16[2,2,256,2048]{3,2,1,0:T(8,128)(2,1)S(1)}, u32[]{:S(2)}) %copy-start.1) | copy-done | bytes 4194328
  79.5 0.4 collective-permute-start
  79.9 0.1 subtract_select_fusion.3
  80.0 0.8 collective-permute-done
  80.8 0.1 broadcast_select_fusion.4
  80.9 0.1 fusion.27
  81.0 0.1 maximum_bitcast_fusion
  81.2 1.1 collective-permute-start.1
  82.3 3.3 %collective-permute-done.1 = f32[2,2,2,2048]{3,1,2,0:T(2,128)S(1)} collective-permute-done((f32[2,2,2,2048]{3,1,2,0:T(2,128)S(1)}, f32[2,2,2,2048]{3,1,2,0:T(2,128)S(1)}, u32[]{:S(2)}, u32[]{:S(2)}) %collective-permute-start.1) | collective-permute-done | bytes 65568 | tf_op jit(solution)/shard_map/ppermute | solution.py:274
  85.6 0.1 copy_select_fusion.2
  85.7 0.1 fusion.23
  86.0 1.1 collective-permute-start.2
  87.2 3.2 %collective-permute-done.2 = f32[2,2,2,2048]{3,1,2,0:T(2,128)S(1)} collective-permute-done((f32[2,2,2,2048]{3,1,2,0:T(2,128)S(1)}, f32[2,2,2,2048]{3,1,2,0:T(2,128)S(1)}, u32[]{:S(2)}, u32[]{:S(2)}) %collective-permute-start.2) | collective-permute-done | bytes 65568 | tf_op jit(solution)/shard_map/ppermute | solution.py:274
  90.4 0.1 copy_select_fusion.1
  90.4 0.1 broadcast_select_fusion.1
  90.5 0.1 fusion.19
  90.8 1.5 %collective-permute-start.3 = (f32[2,2,2,2048]{3,1,2,0:T(2,128)S(1)}, f32[2,2,2,2048]{3,1,2,0:T(2,128)S(1)}, u32[]{:S(2)}, u32[]{:S(2)}) collective-permute-start(f32[2,2,2,2048]{3,1,2,0:T(2,128)S(1)} %copy.20), channel_id=1, source_target_pairs={{0,8},{1,9},{2,10},{3,11},{4,12},{5,13},{6,14},{7,15},{8,0},{9,1},... | collective-permute-start | bytes 196616 | tf_op jit(solution)/shard_map/ppermute | solution.py:274
  92.4 4.4 %collective-permute-done.3 = f32[2,2,2,2048]{3,1,2,0:T(2,128)S(1)} collective-permute-done((f32[2,2,2,2048]{3,1,2,0:T(2,128)S(1)}, f32[2,2,2,2048]{3,1,2,0:T(2,128)S(1)}, u32[]{:S(2)}, u32[]{:S(2)}) %collective-permute-start.3) | collective-permute-done | bytes 65568 | tf_op jit(solution)/shard_map/ppermute | solution.py:274
  96.7 0.1 copy_select_fusion
  96.9 0.1 fusion.13
  97.1 0.2 fusion.10
  97.3 0.2 fusion.11
  97.6 0.2 fusion.9
  97.8 0.2 fusion.8
  98.1 7.8 %solve.1 = bf16[2,2,256,2048]{3,2,1,0:T(8,128)(2,1)S(1)} custom-call(bf16[2,2,256,2048]{3,2,1,0:T(8,128)(2,1)S(1)} %copy-done.2, f32[2,2,2,8,2048]{4,3,2,1,0:T(8,128)S(1)} %get-tuple-element.9.seg_ref, f32[2,2,2,1,2048]{4,3,2,1,0:T(1,128)S(1)} %broadcast_in_dim.13.edge_ref, f32[1,2048]{1,0:T(1,128)S(1)} %bitcast.362, ...), custom_call_target="tpu_custom_call" | custom-call | tf_op jit(solution)/shard_map/solve/pallas_call | solution.py:296
  105.9 13.5 %fusion = f32[2,2,256,2048]{3,2,1,0:T(8,128)} fusion(bf16[2,2,256,2048]{3,2,1,0:T(8,128)(2,1)S(1)} %solve.1, bf16[2048,2048]{1,0:T(8,128)(2,1)} %copy-done), kind=kOutput, calls=%fused_computation | convolution fusion | flops 8589934592 | bytes 20971520 | tf_op jit(solution)/shard_map/rftj,sj->rfts/dot_general | solution.py:310
  (35 shorter events, 0.9 us)
Async XLA Ops:
  0.1 1.0 copy-start.3
  1.2 0.7 copy-start.5
  1.9 60.2 %copy-start.6 = (bf16[2,2,256,2048]{3,2,1,0:T(8,128)(2,1)S(1)}, bf16[2,2,256,2048]{3,2,1,0:T(8,128)(2,1)}, u32[]{:S(2)}) copy-start(bf16[2,2,256,2048]{3,2,1,0:T(8,128)(2,1)} %param.4) | copy-start | bytes 12582916
  62.0 9.2 %copy-start = (bf16[2048,2048]{1,0:T(8,128)(2,1)}, bf16[2048,2048]{1,0:T(8,128)(2,1)S(1)}, u32[]{:S(2)}) copy-start(bf16[2048,2048]{1,0:T(8,128)(2,1)S(1)} %gather_rows.1) | copy-start | bytes 25165828
  62.1 9.2 %copy-start.4 = (f32[2048]{0:T(1024)S(1)}, f32[2048]{0:T(1024)}, u32[]{:S(2)}) copy-start(f32[2048]{0:T(1024)} %param.6) | copy-start | bytes 24580
  77.4 2.0 %copy-start.1 = (bf16[2,2,256,2048]{3,2,1,0:T(8,128)(2,1)}, bf16[2,2,256,2048]{3,2,1,0:T(8,128)(2,1)S(1)}, u32[]{:S(2)}) copy-start(bf16[2,2,256,2048]{3,2,1,0:T(8,128)(2,1)S(1)} %get-tuple-element.8.zp_ref) | copy-start | bytes 12582916
  79.5 1.3 %collective-permute-start = (f32[2,2,2,2048]{3,1,2,0:T(2,128)S(1)}, f32[2,2,2,2048]{3,1,2,0:T(2,128)S(1)}, u32[]{:S(2)}, u32[]{:S(2)}) collective-permute-start(f32[2,2,2,2048]{3,1,2,0:T(2,128)S(1)} %bitcast.364), channel_id=1, source_target_pairs={{0,1},{1,0},{2,3},{3,2},{4,5},{5,4},{6,7},{7,6},{8,9},{9,8},{10,11... | collective-permute-start | bytes 196616 | tf_op jit(solution)/shard_map/ppermute | solution.py:274
  79.9 18.2 %copy-start.2 = (bf16[2,2,256,2048]{3,2,1,0:T(8,128)(2,1)S(1)}, bf16[2,2,256,2048]{3,2,1,0:T(8,128)(2,1)}, u32[]{:S(2)}) copy-start(bf16[2,2,256,2048]{3,2,1,0:T(8,128)(2,1)} %copy-done.1) | copy-start | bytes 12582916
  81.2 4.4 %collective-permute-start.1 = (f32[2,2,2,2048]{3,1,2,0:T(2,128)S(1)}, f32[2,2,2,2048]{3,1,2,0:T(2,128)S(1)}, u32[]{:S(2)}, u32[]{:S(2)}) collective-permute-start(f32[2,2,2,2048]{3,1,2,0:T(2,128)S(1)} %copy.8), channel_id=1, source_target_pairs={{0,2},{1,3},{2,0},{3,1},{4,6},{5,7},{6,4},{7,5},{8,10},{9,11},{10,... | collective-permute-start | bytes 196616 | tf_op jit(solution)/shard_map/ppermute | solution.py:274
  86.0 4.3 %collective-permute-start.2 = (f32[2,2,2,2048]{3,1,2,0:T(2,128)S(1)}, f32[2,2,2,2048]{3,1,2,0:T(2,128)S(1)}, u32[]{:S(2)}, u32[]{:S(2)}) collective-permute-start(f32[2,2,2,2048]{3,1,2,0:T(2,128)S(1)} %copy.14), channel_id=1, source_target_pairs={{0,4},{1,5},{2,6},{3,7},{4,0},{5,1},{6,2},{7,3},{8,12},{9,13},{10,... | collective-permute-start | bytes 196616 | tf_op jit(solution)/shard_map/ppermute | solution.py:274
  90.8 5.9 %collective-permute-start.3 = (f32[2,2,2,2048]{3,1,2,0:T(2,128)S(1)}, f32[2,2,2,2048]{3,1,2,0:T(2,128)S(1)}, u32[]{:S(2)}, u32[]{:S(2)}) collective-permute-start(f32[2,2,2,2048]{3,1,2,0:T(2,128)S(1)} %copy.20), channel_id=1, source_target_pairs={{0,8},{1,9},{2,10},{3,11},{4,12},{5,13},{6,14},{7,15},{8,0},{9,1},... | collective-permute-start | bytes 196616 | tf_op jit(solution)/shard_map/ppermute | solution.py:274

commit v3 on v2

--- a/solution.py
+++ b/solution.py
@@ -126,8 +126,9 @@
 def gather_kernel(chips, mine_ref, node_ref, out_ref, held, send_sem, recv_sem, pair_send, pair_recv):
     _, _, rows, modes = held.shape
     states = out_ref.shape[0]
-    half = modes // 2
-    tile = min(256, states)
+    pieces = 4
+    part = modes // pieces
+    tile = min(512, states)
     me = lax.axis_index("tm")
     core, chip = me % 2, me // 2
     odd = chip % 2
@@ -141,34 +142,41 @@
     targets = (chip_at(place + 1) * 2 + core, chip_at(place - 1) * 2 + core)
     pair = chip * 2 + 1 - core
 
-    def piece(step, h):
-        source = chip_at(place - step if h == 0 else place + step)
-        return source, held.at[source, core, :, pl.ds(h * half, half)]
-
-    def ring(step, h):
-        _, ref = piece(step, h)
+    def piece(step, i):
+        source = chip_at(place - step if i % 2 == 0 else place + step)
+        return source, held.at[source, core, :, pl.ds(i * part, part)]
+
+    def ring(step, i):
+        _, ref = piece(step, i)
         return pltpu.make_async_remote_copy(
-            src_ref=ref, dst_ref=ref, send_sem=send_sem.at[step, h], recv_sem=recv_sem.at[step, h],
-            device_id={"tm": targets[h]}, device_id_type=pl.DeviceIdType.MESH,
+            src_ref=ref, dst_ref=ref, send_sem=send_sem.at[step, i], recv_sem=recv_sem.at[step, i],
+            device_id={"tm": targets[i % 2]}, device_id_type=pl.DeviceIdType.MESH,
         )
 
-    def share(step, h):
-        _, ref = piece(step, h)
+    def landed(step, i):
+        _, ref = piece(step + 1, i)
         return pltpu.make_async_remote_copy(
-            src_ref=ref, dst_ref=ref, send_sem=pair_send.at[step, h], recv_sem=pair_recv.at[step, h],
+            src_ref=ref, dst_ref=ref, send_sem=send_sem.at[step, i], recv_sem=recv_sem.at[step, i],
+            device_id={"tm": targets[i % 2]}, device_id_type=pl.DeviceIdType.MESH,
+        )
+
+    def share(step, i):
+        _, ref = piece(step, i)
+        return pltpu.make_async_remote_copy(
+            src_ref=ref, dst_ref=ref, send_sem=pair_send.at[step, i], recv_sem=pair_recv.at[step, i],
             device_id={"tm": pair}, device_id_type=pl.DeviceIdType.MESH,
         )
 
-    def place_rows(step, h, first):
-        source, _ = piece(step, h)
+    def place_rows(step, i, first):
+        source, _ = piece(step, i)
         nodes = node_ref[source]
-        columns = pl.ds(h * half, half)
+        columns = pl.ds(i * part, part)
 
         def one_tile(t, carry):
             start = pl.multiple_of(t * tile, tile)
             index = lax.broadcasted_iota(jnp.int32, (tile, 2 * rows), 0) + start
             choose = jnp.where(index == nodes, 1.0, 0.0).astype(jnp.bfloat16)
-            block = held[source, :, :, columns].reshape(2 * rows, half)
+            block = held[source, :, :, columns].reshape(2 * rows, part)
             moved = jnp.dot(choose, block, preferred_element_type=jnp.float32)
             here = pl.ds(start, tile)
             if not first:
@@ -184,29 +192,39 @@
         pl.semaphore_signal(barrier, inc=1, device_id={"tm": target}, device_id_type=pl.DeviceIdType.MESH)
     pl.semaphore_wait(barrier, 3)
 
-    def one_step(step, first):
-        for h in range(2):
-            ring(step, h).start()
-        for h in range(2):
-            share(step, h).start()
-        for h in range(2):
-            share(step, h).wait()
-            place_rows(step, h, first)
-        for h in range(2):
-            ring(step, h).wait()
-
-    one_step(0, True)
+    def one_step(step, first, last):
+        for i in range(pieces):
+            landed(step - 1, i).wait_recv()
+            if not last:
+                ring(step, i).start()
+            share(step, i).start()
+            share(step - 1, i).wait_recv()
+            place_rows(step - 1, i, first)
+
+    for i in range(pieces):
+        ring(0, i).start()
+        share(0, i).start()
+    one_step(1, True, False)
 
     def body(step, carry):
-        one_step(step, False)
+        one_step(step, False, False)
         return carry
 
-    lax.fori_loop(1, chips - 1, body, 0)
-    for h in range(2):
-        share(chips - 1, h).start()
-    for h in range(2):
-        share(chips - 1, h).wait()
-        place_rows(chips - 1, h, False)
+    lax.fori_loop(2, chips - 1, body, 0)
+    one_step(chips - 1, False, True)
+    for i in range(pieces):
+        share(chips - 1, i).wait_recv()
+        place_rows(chips - 1, i, False)
+
+    def drain(step, carry):
+        for i in range(pieces):
+            ring(step, i).wait_send()
+            share(step, i).wait_send()
+        return carry
+
+    lax.fori_loop(0, chips - 1, drain, 0)
+    for i in range(pieces):
+        share(chips - 1, i).wait_send()
 
 
 def on_device(residual, eigenbasis, eigenvalues, node_order):
@@ -226,7 +244,7 @@
         in_specs=[pl.BlockSpec(memory_space=pltpu.VMEM)] * 2,
         out_specs=pl.BlockSpec(memory_space=pltpu.VMEM),
         scratch_shapes=[pltpu.VMEM((chips, 2, rows, modes), jnp.bfloat16)]
-        + [pltpu.SemaphoreType.DMA((chips, 2))] * 4,
+        + [pltpu.SemaphoreType.DMA((chips, 4))] * 4,
         compiler_params=pltpu.CompilerParams(
             collective_id=0, has_side_effects=True, vmem_limit_bytes=44 * 1024 * 1024
         ),

time: 120 us -> 113 us (0.942)
  Pallas kernels: 74 us -> 67.9 us
    pallas_call x1, Pallas kernels: 60.2 us -> 53.8 us  [on_device(): pl.pallas_call(functools.partial(gather_kernel, chips), out_shape=jax.Sha...]
where the time goes in v3:
time: 113 us
  Pallas kernels  67.9 us (60%)
  matrix products  22.5 us (20%)
  waiting for transfers between devices  11.2 us (10%)
  starting transfers between devices  4.43 us (4%)
  local copies, waits for them, and re-layouts  4.04 us (4%)
  other arithmetic  2.43 us (2%)
    pallas_call x1, Pallas kernels, on_device(): pl.pallas_call(functools.partial(gather_kernel, chips), out_shape=jax.Sha...  53.8 us
    dot_general x1, matrix products, on_device(): jnp.einsum('rftj,sj->rfts', back, basis, preferred_element_type=jnp.float32)  13.3 us
    ppermute x4, waiting for transfers between devices, on_device(): other = lax.ppermute(group, 'tm', [(d, d ^ reach) for d in range(parts)])  11.2 us
    dot_general x1, matrix products, on_device(): jnp.einsum('rfts,sj->rftj', residual, basis, preferred_element_type=jnp.f...  9.21 us
    pallas_call x1, Pallas kernels, on_device(): pl.pallas_call(solve_kernel, grid=(blocks,), in_specs=[wide_block, seg_bl...  7.78 us
    pallas_call x1, Pallas kernels, on_device(): pl.pallas_call(carries_kernel, grid=(blocks,), in_specs=[wide_block, mu_b...  6.27 us
    ppermute x4, starting transfers between devices, on_device(): other = lax.ppermute(group, 'tm', [(d, d ^ reach) for d in range(parts)])  4.43 us
    unnamed x14, local copies, waits for them, and re-layouts  3.76 us
  transfers between devices with their start and end apart: 4, of which 4 were waited for; matrix products, arithmetic and copies ran while one was open for 0% of the time, Pallas kernels for 0%

profile of v3, /device:TPU:0, one launch (start us, length us, event | category | flops | bytes accessed | tf_op | source)
XLA Modules:
  0.0 112.9 jit_solution(10597479560934683214)
XLA Ops:
  0.0 0.1 fusion.7
  0.1 1.0 copy-done.3
  1.2 0.7 copy-done.5
  1.9 53.8 %gather_rows.1 = bf16[2048,2048]{1,0:T(8,128)(2,1)S(1)} custom-call(bf16[128,2048]{1,0:T(8,128)(2,1)S(1)} %copy-done.3, s32[8,1,256]{2,1,0:T(1,128)S(1)} %bitcast.363), custom_call_target="tpu_custom_call" | custom-call | tf_op jit(solution)/shard_map/gather_rows/pallas_call | solution.py:241
  55.7 9.2 %convert_bitcast_fusion.modal_ref = bf16[2,2,256,2048]{3,2,1,0:T(8,128)(2,1)S(1)} fusion(bf16[2,2,256,2048]{3,2,1,0:T(8,128)(2,1)S(1)} %copy-done.6, bf16[2048,2048]{1,0:T(8,128)(2,1)S(1)} %gather_rows.1), kind=kOutput, calls=%fused_computation.4 | convolution fusion | flops 8592031744 | bytes 16777216 | tf_op jit(solution)/shard_map/rfts,sj->rftj/dot_general | solution.py:254
  65.0 6.3 %carries.1 = (bf16[2,2,256,2048]{3,2,1,0:T(8,128)(2,1)S(1)}, f32[2,2,2,8,2048]{4,3,2,1,0:T(8,128)S(1)}, f32[2,2,2,1,2048]{4,3,2,1,0:T(1,128)S(1)}) custom-call(bf16[2,2,256,2048]{3,2,1,0:T(8,128)(2,1)S(1)} %convert_bitcast_fusion.modal_ref, f32[1,2048]{1,0:T(1,128)S(1)} %bitcast.361, bf16[256,256]{1,0:T(8,128)(2,1)S(1)} %get-tuple-element.62.perm_ref), custom_call_target="tpu_custom_call" | custom-call | tf_op jit(solution)/shard_map/carries/pallas_call | solution.py:268
  71.3 2.0 %copy-done.1 = bf16[2,2,256,2048]{3,2,1,0:T(8,128)(2,1)} copy-done((bf16[2,2,256,2048]{3,2,1,0:T(8,128)(2,1)}, bf16[2,2,256,2048]{3,2,1,0:T(8,128)(2,1)S(1)}, u32[]{:S(2)}) %copy-start.1) | copy-done | bytes 4194328
  73.3 0.1 collective-permute-start
  73.5 0.1 subtract_select_fusion.3
  73.6 1.1 collective-permute-done
  74.6 0.1 broadcast_select_fusion.4
  74.7 0.1 fusion.27
  74.8 0.1 maximum_bitcast_fusion
  75.0 1.7 %collective-permute-start.1 = (f32[2,2,2,2048]{3,1,2,0:T(2,128)S(1)}, f32[2,2,2,2048]{3,1,2,0:T(2,128)S(1)}, u32[]{:S(2)}, u32[]{:S(2)}) collective-permute-start(f32[2,2,2,2048]{3,1,2,0:T(2,128)S(1)} %copy.8), channel_id=1, source_target_pairs={{0,2},{1,3},{2,0},{3,1},{4,6},{5,7},{6,4},{7,5},{8,10},{9,11},{10,... | collective-permute-start | bytes 196616 | tf_op jit(solution)/shard_map/ppermute | solution.py:292
  76.7 2.7 %collective-permute-done.1 = f32[2,2,2,2048]{3,1,2,0:T(2,128)S(1)} collective-permute-done((f32[2,2,2,2048]{3,1,2,0:T(2,128)S(1)}, f32[2,2,2,2048]{3,1,2,0:T(2,128)S(1)}, u32[]{:S(2)}, u32[]{:S(2)}) %collective-permute-start.1) | collective-permute-done | bytes 65568 | tf_op jit(solution)/shard_map/ppermute | solution.py:292
  79.3 0.1 copy_select_fusion.2
  79.4 0.1 broadcast_select_fusion.2
  79.5 0.1 fusion.23
  79.8 1.1 collective-permute-start.2
  80.9 3.2 %collective-permute-done.2 = f32[2,2,2,2048]{3,1,2,0:T(2,128)S(1)} collective-permute-done((f32[2,2,2,2048]{3,1,2,0:T(2,128)S(1)}, f32[2,2,2,2048]{3,1,2,0:T(2,128)S(1)}, u32[]{:S(2)}, u32[]{:S(2)}) %collective-permute-start.2) | collective-permute-done | bytes 65568 | tf_op jit(solution)/shard_map/ppermute | solution.py:292
  84.1 0.1 copy_select_fusion.1
  84.3 0.1 fusion.19
  84.6 1.6 %collective-permute-start.3 = (f32[2,2,2,2048]{3,1,2,0:T(2,128)S(1)}, f32[2,2,2,2048]{3,1,2,0:T(2,128)S(1)}, u32[]{:S(2)}, u32[]{:S(2)}) collective-permute-start(f32[2,2,2,2048]{3,1,2,0:T(2,128)S(1)} %copy.20), channel_id=1, source_target_pairs={{0,8},{1,9},{2,10},{3,11},{4,12},{5,13},{6,14},{7,15},{8,0},{9,1},... | collective-permute-start | bytes 196616 | tf_op jit(solution)/shard_map/ppermute | solution.py:292
  86.2 4.3 %collective-permute-done.3 = f32[2,2,2,2048]{3,1,2,0:T(2,128)S(1)} collective-permute-done((f32[2,2,2,2048]{3,1,2,0:T(2,128)S(1)}, f32[2,2,2,2048]{3,1,2,0:T(2,128)S(1)}, u32[]{:S(2)}, u32[]{:S(2)}) %collective-permute-start.3) | collective-permute-done | bytes 65568 | tf_op jit(solution)/shard_map/ppermute | solution.py:292
  90.5 0.1 copy_select_fusion
  90.6 0.1 fusion.13
  90.9 0.2 fusion.10
  91.1 0.2 fusion.11
  91.3 0.2 fusion.9
  91.5 0.2 fusion.8
  91.9 7.8 %solve.1 = bf16[2,2,256,2048]{3,2,1,0:T(8,128)(2,1)S(1)} custom-call(bf16[2,2,256,2048]{3,2,1,0:T(8,128)(2,1)S(1)} %copy-done.2, f32[2,2,2,8,2048]{4,3,2,1,0:T(8,128)S(1)} %get-tuple-element.9.seg_ref, f32[2,2,2,1,2048]{4,3,2,1,0:T(1,128)S(1)} %broadcast_in_dim.13.edge_ref, f32[1,2048]{1,0:T(1,128)S(1)} %bitcast.362, ...), custom_call_target="tpu_custom_call" | custom-call | tf_op jit(solution)/shard_map/solve/pallas_call | solution.py:314
  99.7 13.3 %fusion = f32[2,2,256,2048]{3,2,1,0:T(8,128)} fusion(bf16[2,2,256,2048]{3,2,1,0:T(8,128)(2,1)S(1)} %solve.1, bf16[2048,2048]{1,0:T(8,128)(2,1)} %copy-done), kind=kOutput, calls=%fused_computation | convolution fusion | flops 8589934592 | bytes 20971520 | tf_op jit(solution)/shard_map/rftj,sj->rfts/dot_general | solution.py:328
  (35 shorter events, 0.9 us)
Async XLA Ops:
  0.1 1.0 copy-start.3
  1.2 0.7 copy-start.5
  1.9 53.8 %copy-start.6 = (bf16[2,2,256,2048]{3,2,1,0:T(8,128)(2,1)S(1)}, bf16[2,2,256,2048]{3,2,1,0:T(8,128)(2,1)}, u32[]{:S(2)}) copy-start(bf16[2,2,256,2048]{3,2,1,0:T(8,128)(2,1)} %param.4) | copy-start | bytes 12582916
  55.7 9.2 %copy-start = (bf16[2048,2048]{1,0:T(8,128)(2,1)}, bf16[2048,2048]{1,0:T(8,128)(2,1)S(1)}, u32[]{:S(2)}) copy-start(bf16[2048,2048]{1,0:T(8,128)(2,1)S(1)} %gather_rows.1) | copy-start | bytes 25165828
  55.7 9.2 %copy-start.4 = (f32[2048]{0:T(1024)S(1)}, f32[2048]{0:T(1024)}, u32[]{:S(2)}) copy-start(f32[2048]{0:T(1024)} %param.6) | copy-start | bytes 24580
  71.2 2.0 %copy-start.1 = (bf16[2,2,256,2048]{3,2,1,0:T(8,128)(2,1)}, bf16[2,2,256,2048]{3,2,1,0:T(8,128)(2,1)S(1)}, u32[]{:S(2)}) copy-start(bf16[2,2,256,2048]{3,2,1,0:T(8,128)(2,1)S(1)} %get-tuple-element.8.zp_ref) | copy-start | bytes 12582916
  73.3 1.3 %collective-permute-start = (f32[2,2,2,2048]{3,1,2,0:T(2,128)S(1)}, f32[2,2,2,2048]{3,1,2,0:T(2,128)S(1)}, u32[]{:S(2)}, u32[]{:S(2)}) collective-permute-start(f32[2,2,2,2048]{3,1,2,0:T(2,128)S(1)} %bitcast.364), channel_id=1, source_target_pairs={{0,1},{1,0},{2,3},{3,2},{4,5},{5,4},{6,7},{7,6},{8,9},{9,8},{10,11... | collective-permute-start | bytes 196616 | tf_op jit(solution)/shard_map/ppermute | solution.py:292
  73.5 18.4 %copy-start.2 = (bf16[2,2,256,2048]{3,2,1,0:T(8,128)(2,1)S(1)}, bf16[2,2,256,2048]{3,2,1,0:T(8,128)(2,1)}, u32[]{:S(2)}) copy-start(bf16[2,2,256,2048]{3,2,1,0:T(8,128)(2,1)} %copy-done.1) | copy-start | bytes 12582916
  75.0 4.3 %collective-permute-start.1 = (f32[2,2,2,2048]{3,1,2,0:T(2,128)S(1)}, f32[2,2,2,2048]{3,1,2,0:T(2,128)S(1)}, u32[]{:S(2)}, u32[]{:S(2)}) collective-permute-start(f32[2,2,2,2048]{3,1,2,0:T(2,128)S(1)} %copy.8), channel_id=1, source_target_pairs={{0,2},{1,3},{2,0},{3,1},{4,6},{5,7},{6,4},{7,5},{8,10},{9,11},{10,... | collective-permute-start | bytes 196616 | tf_op jit(solution)/shard_map/ppermute | solution.py:292
  79.8 4.3 %collective-permute-start.2 = (f32[2,2,2,2048]{3,1,2,0:T(2,128)S(1)}, f32[2,2,2,2048]{3,1,2,0:T(2,128)S(1)}, u32[]{:S(2)}, u32[]{:S(2)}) collective-permute-start(f32[2,2,2,2048]{3,1,2,0:T(2,128)S(1)} %copy.14), channel_id=1, source_target_pairs={{0,4},{1,5},{2,6},{3,7},{4,0},{5,1},{6,2},{7,3},{8,12},{9,13},{10,... | collective-permute-start | bytes 196616 | tf_op jit(solution)/shard_map/ppermute | solution.py:292
  84.6 5.9 %collective-permute-start.3 = (f32[2,2,2,2048]{3,1,2,0:T(2,128)S(1)}, f32[2,2,2,2048]{3,1,2,0:T(2,128)S(1)}, u32[]{:S(2)}, u32[]{:S(2)}) collective-permute-start(f32[2,2,2,2048]{3,1,2,0:T(2,128)S(1)} %copy.20), channel_id=1, source_target_pairs={{0,8},{1,9},{2,10},{3,11},{4,12},{5,13},{6,14},{7,15},{8,0},{9,1},... | collective-permute-start | bytes 196616 | tf_op jit(solution)/shard_map/ppermute | solution.py:292

commit v4 on v3

--- a/solution.py
+++ b/solution.py
@@ -168,20 +168,21 @@
         )
 
     def place_rows(step, i, first):
+        if i < 2:
+            return
         source, _ = piece(step, i)
         nodes = node_ref[source]
-        columns = pl.ds(i * part, part)
 
         def one_tile(t, carry):
             start = pl.multiple_of(t * tile, tile)
             index = lax.broadcasted_iota(jnp.int32, (tile, 2 * rows), 0) + start
             choose = jnp.where(index == nodes, 1.0, 0.0).astype(jnp.bfloat16)
-            block = held[source, :, :, columns].reshape(2 * rows, part)
-            moved = jnp.dot(choose, block, preferred_element_type=jnp.float32)
             here = pl.ds(start, tile)
-            if not first:
-                moved = moved + out_ref[here, columns].astype(jnp.float32)
-            out_ref[here, columns] = moved.astype(jnp.bfloat16)
+            for c in (i - 2, i):
+                columns = pl.ds(c * part, part)
+                block = held[source, :, :, columns].reshape(2 * rows, part)
+                moved = jnp.dot(choose, block, preferred_element_type=jnp.float32).astype(jnp.bfloat16)
+                out_ref[here, columns] = moved if first else moved + out_ref[here, columns]
             return carry
 
         lax.fori_loop(0, states // tile, one_tile, 0)

time: 113 us -> 113 us (level)
  no operation moved by 1% of the time
where the time goes in v4:
time: 113 us
  Pallas kernels  67.5 us (60%)
  matrix products  22.5 us (20%)
  waiting for transfers between devices  12.3 us (11%)
  local copies, waits for them, and re-layouts  4.04 us (4%)
  starting transfers between devices  3.41 us (3%)
  other arithmetic  2.43 us (2%)
    pallas_call x1, Pallas kernels, on_device(): pl.pallas_call(functools.partial(gather_kernel, chips), out_shape=jax.Sha...  53.5 us
    dot_general x1, matrix products, on_device(): jnp.einsum('rftj,sj->rfts', back, basis, preferred_element_type=jnp.float32)  13.3 us
    ppermute x4, waiting for transfers between devices, on_device(): other = lax.ppermute(group, 'tm', [(d, d ^ reach) for d in range(parts)])  12.3 us
    dot_general x1, matrix products, on_device(): jnp.einsum('rfts,sj->rftj', residual, basis, preferred_element_type=jnp.f...  9.21 us
    pallas_call x1, Pallas kernels, on_device(): pl.pallas_call(solve_kernel, grid=(blocks,), in_specs=[wide_block, seg_bl...  7.78 us
    pallas_call x1, Pallas kernels, on_device(): pl.pallas_call(carries_kernel, grid=(blocks,), in_specs=[wide_block, mu_b...  6.27 us
    unnamed x14, local copies, waits for them, and re-layouts  3.76 us
    ppermute x4, starting transfers between devices, on_device(): other = lax.ppermute(group, 'tm', [(d, d ^ reach) for d in range(parts)])  3.41 us
  transfers between devices with their start and end apart: 4, of which 4 were waited for; matrix products, arithmetic and copies ran while one was open for 0% of the time, Pallas kernels for 0%

profile of v4, /device:TPU:0, one launch (start us, length us, event | category | flops | bytes accessed | tf_op | source)
XLA Modules:
  0.0 112.6 jit_solution(9756642453571122671)
XLA Ops:
  0.0 0.1 fusion.7
  0.1 1.0 copy-done.3
  1.2 0.7 copy-done.5
  1.9 53.5 %gather_rows.1 = bf16[2048,2048]{1,0:T(8,128)(2,1)S(1)} custom-call(bf16[128,2048]{1,0:T(8,128)(2,1)S(1)} %copy-done.3, s32[8,1,256]{2,1,0:T(1,128)S(1)} %bitcast.363), custom_call_target="tpu_custom_call" | custom-call | tf_op jit(solution)/shard_map/gather_rows/pallas_call | solution.py:242
  55.4 9.2 %convert_bitcast_fusion.modal_ref = bf16[2,2,256,2048]{3,2,1,0:T(8,128)(2,1)S(1)} fusion(bf16[2,2,256,2048]{3,2,1,0:T(8,128)(2,1)S(1)} %copy-done.6, bf16[2048,2048]{1,0:T(8,128)(2,1)S(1)} %gather_rows.1), kind=kOutput, calls=%fused_computation.4 | convolution fusion | flops 8592031744 | bytes 16777216 | tf_op jit(solution)/shard_map/rfts,sj->rftj/dot_general | solution.py:255
  64.6 6.3 %carries.1 = (bf16[2,2,256,2048]{3,2,1,0:T(8,128)(2,1)S(1)}, f32[2,2,2,8,2048]{4,3,2,1,0:T(8,128)S(1)}, f32[2,2,2,1,2048]{4,3,2,1,0:T(1,128)S(1)}) custom-call(bf16[2,2,256,2048]{3,2,1,0:T(8,128)(2,1)S(1)} %convert_bitcast_fusion.modal_ref, f32[1,2048]{1,0:T(1,128)S(1)} %bitcast.361, bf16[256,256]{1,0:T(8,128)(2,1)S(1)} %get-tuple-element.62.perm_ref), custom_call_target="tpu_custom_call" | custom-call | tf_op jit(solution)/shard_map/carries/pallas_call | solution.py:269
  70.9 2.0 %copy-done.1 = bf16[2,2,256,2048]{3,2,1,0:T(8,128)(2,1)} copy-done((bf16[2,2,256,2048]{3,2,1,0:T(8,128)(2,1)}, bf16[2,2,256,2048]{3,2,1,0:T(8,128)(2,1)S(1)}, u32[]{:S(2)}) %copy-start.1) | copy-done | bytes 4194328
  73.0 0.1 collective-permute-start
  73.2 0.1 subtract_select_fusion.3
  73.2 1.1 collective-permute-done
  74.3 0.1 broadcast_select_fusion.4
  74.4 0.1 fusion.27
  74.5 0.1 maximum_bitcast_fusion
  74.7 1.4 %collective-permute-start.1 = (f32[2,2,2,2048]{3,1,2,0:T(2,128)S(1)}, f32[2,2,2,2048]{3,1,2,0:T(2,128)S(1)}, u32[]{:S(2)}, u32[]{:S(2)}) collective-permute-start(f32[2,2,2,2048]{3,1,2,0:T(2,128)S(1)} %copy.8), channel_id=1, source_target_pairs={{0,2},{1,3},{2,0},{3,1},{4,6},{5,7},{6,4},{7,5},{8,10},{9,11},{10,... | collective-permute-start | bytes 196616 | tf_op jit(solution)/shard_map/ppermute | solution.py:293
  76.1 2.9 %collective-permute-done.1 = f32[2,2,2,2048]{3,1,2,0:T(2,128)S(1)} collective-permute-done((f32[2,2,2,2048]{3,1,2,0:T(2,128)S(1)}, f32[2,2,2,2048]{3,1,2,0:T(2,128)S(1)}, u32[]{:S(2)}, u32[]{:S(2)}) %collective-permute-start.1) | collective-permute-done | bytes 65568 | tf_op jit(solution)/shard_map/ppermute | solution.py:293
  79.0 0.1 copy_select_fusion.2
  79.1 0.1 broadcast_select_fusion.2
  79.1 0.1 fusion.23
  79.4 0.8 collective-permute-start.2
  80.3 3.5 %collective-permute-done.2 = f32[2,2,2,2048]{3,1,2,0:T(2,128)S(1)} collective-permute-done((f32[2,2,2,2048]{3,1,2,0:T(2,128)S(1)}, f32[2,2,2,2048]{3,1,2,0:T(2,128)S(1)}, u32[]{:S(2)}, u32[]{:S(2)}) %collective-permute-start.2) | collective-permute-done | bytes 65568 | tf_op jit(solution)/shard_map/ppermute | solution.py:293
  83.8 0.1 copy_select_fusion.1
  83.9 0.1 fusion.19
  84.2 1.1 collective-permute-start.3
  85.3 4.8 %collective-permute-done.3 = f32[2,2,2,2048]{3,1,2,0:T(2,128)S(1)} collective-permute-done((f32[2,2,2,2048]{3,1,2,0:T(2,128)S(1)}, f32[2,2,2,2048]{3,1,2,0:T(2,128)S(1)}, u32[]{:S(2)}, u32[]{:S(2)}) %collective-permute-start.3) | collective-permute-done | bytes 65568 | tf_op jit(solution)/shard_map/ppermute | solution.py:293
  90.2 0.1 copy_select_fusion
  90.3 0.1 fusion.13
  90.5 0.2 fusion.10
  90.8 0.2 fusion.11
  91.0 0.2 fusion.9
  91.2 0.2 fusion.8
  91.5 7.8 %solve.1 = bf16[2,2,256,2048]{3,2,1,0:T(8,128)(2,1)S(1)} custom-call(bf16[2,2,256,2048]{3,2,1,0:T(8,128)(2,1)S(1)} %copy-done.2, f32[2,2,2,8,2048]{4,3,2,1,0:T(8,128)S(1)} %get-tuple-element.9.seg_ref, f32[2,2,2,1,2048]{4,3,2,1,0:T(1,128)S(1)} %broadcast_in_dim.13.edge_ref, f32[1,2048]{1,0:T(1,128)S(1)} %bitcast.362, ...), custom_call_target="tpu_custom_call" | custom-call | tf_op jit(solution)/shard_map/solve/pallas_call | solution.py:315
  99.3 13.3 %fusion = f32[2,2,256,2048]{3,2,1,0:T(8,128)} fusion(bf16[2,2,256,2048]{3,2,1,0:T(8,128)(2,1)S(1)} %solve.1, bf16[2048,2048]{1,0:T(8,128)(2,1)} %copy-done), kind=kOutput, calls=%fused_computation | convolution fusion | flops 8589934592 | bytes 20971520 | tf_op jit(solution)/shard_map/rftj,sj->rfts/dot_general | solution.py:329
  (35 shorter events, 0.9 us)
Async XLA Ops:
  0.1 1.0 copy-start.3
  1.2 0.7 copy-start.5
  1.9 53.5 %copy-start.6 = (bf16[2,2,256,2048]{3,2,1,0:T(8,128)(2,1)S(1)}, bf16[2,2,256,2048]{3,2,1,0:T(8,128)(2,1)}, u32[]{:S(2)}) copy-start(bf16[2,2,256,2048]{3,2,1,0:T(8,128)(2,1)} %param.4) | copy-start | bytes 12582916
  55.4 9.2 %copy-start = (bf16[2048,2048]{1,0:T(8,128)(2,1)}, bf16[2048,2048]{1,0:T(8,128)(2,1)S(1)}, u32[]{:S(2)}) copy-start(bf16[2048,2048]{1,0:T(8,128)(2,1)S(1)} %gather_rows.1) | copy-start | bytes 25165828
  55.4 9.2 %copy-start.4 = (f32[2048]{0:T(1024)S(1)}, f32[2048]{0:T(1024)}, u32[]{:S(2)}) copy-start(f32[2048]{0:T(1024)} %param.6) | copy-start | bytes 24580
  70.9 2.0 %copy-start.1 = (bf16[2,2,256,2048]{3,2,1,0:T(8,128)(2,1)}, bf16[2,2,256,2048]{3,2,1,0:T(8,128)(2,1)S(1)}, u32[]{:S(2)}) copy-start(bf16[2,2,256,2048]{3,2,1,0:T(8,128)(2,1)S(1)} %get-tuple-element.8.zp_ref) | copy-start | bytes 12582916
  73.0 1.3 %collective-permute-start = (f32[2,2,2,2048]{3,1,2,0:T(2,128)S(1)}, f32[2,2,2,2048]{3,1,2,0:T(2,128)S(1)}, u32[]{:S(2)}, u32[]{:S(2)}) collective-permute-start(f32[2,2,2,2048]{3,1,2,0:T(2,128)S(1)} %bitcast.364), channel_id=1, source_target_pairs={{0,1},{1,0},{2,3},{3,2},{4,5},{5,4},{6,7},{7,6},{8,9},{9,8},{10,11... | collective-permute-start | bytes 196616 | tf_op jit(solution)/shard_map/ppermute | solution.py:293
  73.1 18.4 %copy-start.2 = (bf16[2,2,256,2048]{3,2,1,0:T(8,128)(2,1)S(1)}, bf16[2,2,256,2048]{3,2,1,0:T(8,128)(2,1)}, u32[]{:S(2)}) copy-start(bf16[2,2,256,2048]{3,2,1,0:T(8,128)(2,1)} %copy-done.1) | copy-start | bytes 12582916
  74.7 4.3 %collective-permute-start.1 = (f32[2,2,2,2048]{3,1,2,0:T(2,128)S(1)}, f32[2,2,2,2048]{3,1,2,0:T(2,128)S(1)}, u32[]{:S(2)}, u32[]{:S(2)}) collective-permute-start(f32[2,2,2,2048]{3,1,2,0:T(2,128)S(1)} %copy.8), channel_id=1, source_target_pairs={{0,2},{1,3},{2,0},{3,1},{4,6},{5,7},{6,4},{7,5},{8,10},{9,11},{10,... | collective-permute-start | bytes 196616 | tf_op jit(solution)/shard_map/ppermute | solution.py:293
  79.4 4.3 %collective-permute-start.2 = (f32[2,2,2,2048]{3,1,2,0:T(2,128)S(1)}, f32[2,2,2,2048]{3,1,2,0:T(2,128)S(1)}, u32[]{:S(2)}, u32[]{:S(2)}) collective-permute-start(f32[2,2,2,2048]{3,1,2,0:T(2,128)S(1)} %copy.14), channel_id=1, source_target_pairs={{0,4},{1,5},{2,6},{3,7},{4,0},{5,1},{6,2},{7,3},{8,12},{9,13},{10,... | collective-permute-start | bytes 196616 | tf_op jit(solution)/shard_map/ppermute | solution.py:293
  84.2 5.9 %collective-permute-start.3 = (f32[2,2,2,2048]{3,1,2,0:T(2,128)S(1)}, f32[2,2,2,2048]{3,1,2,0:T(2,128)S(1)}, u32[]{:S(2)}, u32[]{:S(2)}) collective-permute-start(f32[2,2,2,2048]{3,1,2,0:T(2,128)S(1)} %copy.20), channel_id=1, source_target_pairs={{0,8},{1,9},{2,10},{3,11},{4,12},{5,13},{6,14},{7,15},{8,0},{9,1},... | collective-permute-start | bytes 196616 | tf_op jit(solution)/shard_map/ppermute | solution.py:293
